TPU v7x, 32 devices: a whole 2x2x4 slice. The times are simulated.
32 devices in a mesh: groups: 2 (over y), dp: 16 (over z, x, core).
Axes of the slice: x: 2, y: 2, z: 4, core: 2. Of those that a mesh axis runs over, the one named last changes fastest.
Arguments:
- tokens: bfloat16 [256, 8192], P(('groups', 'dp')), parts along dimension 0, may hold values from -6 to 6
- token_adapter_index: int32 [256, 1], P(('groups', 'dp')), parts along dimension 0, may hold values from 0 to 15; in each aligned block of 128 rows (0 to 127, 128 to 255, ...) at most 32 rows name the same one
- adapter_slot_index: int32 [16], replicated, may hold values from 0 to 15, each once
- gate_matrix: bfloat16 [8192, 28672], P(None, 'dp'), may hold values from -0.0625 to 0.0625
- up_matrix: bfloat16 [8192, 28672], P(None, 'dp'), may hold values from -0.0625 to 0.0625
- adapter_down_factor: bfloat16 [16, 8192, 64], P('dp'), may hold values from -0.0625 to 0.0625
- adapter_up_factor: bfloat16 [16, 64, 28672], P('dp'), may hold values from -0.75 to 0.75
Outputs:
- hidden: bfloat16 [256, 28672], P('groups', 'dp'), parts along dimension 0
There are 2 independent parts, one for each index of `groups`. A program takes and returns all parts, laid end to end along the dimension named above; an argument that names none is the same for every part. Nothing has to cross between parts.
Inputs may be any that keep to these rules, and one draw needn't show every extreme that they name: `token_adapter_index`: no adapter is named by more than 32 rows of a group, and one is named by exactly 32. `adapter_slot_index`: each slot holds exactly one adapter.
All inputs are finite; a program needn't handle non-finite values.
Results may differ from a plain program's by a relative error of at most 0.0075.
Values may be sent and summed in bfloat16 or wider, within the bound.
No kernel may reach another device: no remote copies, remote signals or barrier semaphores. Data moves between devices by JAX's collectives and lax.ppermute only.
A program may use at most 192 MiB of HBM per device.

v0:
```python
import jax
import jax.numpy as jnp
from jax import lax
from jax.sharding import PartitionSpec as P

CAP = 32


def shards(
    tokens,
    token_adapter_index,
    adapter_slot_index,
    gate_matrix,
    up_matrix,
    adapter_down_factor,
    adapter_up_factor,
):
    count = lax.axis_size("dp")
    myself = lax.axis_index("dp")
    all_rows, all_ids = (
        lax.all_gather(tokens, "dp", axis=0, tiled=True),
        lax.all_gather(token_adapter_index, "dp", axis=0, tiled=True),
    )
    total = all_rows.shape[0]
    places = jnp.arange(count, dtype=jnp.int32)
    match = all_ids[:, 0][:, None] == places[None, :]
    slots = jnp.sum(jnp.where(match, adapter_slot_index[None, :], 0), 1)
    slot_match = slots[:, None] == places[None, :]
    onehot = slot_match.astype(jnp.int32)
    ranks = jnp.sum(jnp.cumsum(onehot, 0) * onehot, 1) - 1
    capacity = CAP
    columns = jnp.arange(capacity, dtype=jnp.int32)
    mine = (slots == myself)[:, None] & (ranks[:, None] == columns[None, :])
    row_list = jnp.sum(jnp.where(mine, jnp.arange(total, dtype=jnp.int32)[:, None], 0), 0)
    selected_slot = jnp.take(all_rows, row_list, axis=0)
    reduced_rows = jnp.dot(
        selected_slot, adapter_down_factor[0], preferred_element_type=jnp.float32
    ).astype(jnp.bfloat16)
    slot_pieces = lax.all_to_all(adapter_up_factor, "dp", split_axis=2, concat_axis=0, tiled=True)
    all_low = lax.all_gather(reduced_rows, "dp", axis=0, tiled=True)
    rank_width = all_low.shape[1]
    token_low = jnp.take(all_low, slots * capacity + ranks, axis=0)
    expanded = (token_low[:, None, :] * slot_match.astype(jnp.bfloat16)[:, :, None]).reshape(
        total, count * rank_width
    )
    stacked = slot_pieces.reshape(count * rank_width, slot_pieces.shape[2])
    delta = jnp.dot(expanded, stacked, preferred_element_type=jnp.float32).astype(jnp.bfloat16)
    gate_base = jnp.dot(all_rows, gate_matrix, preferred_element_type=jnp.float32)
    up = jnp.dot(all_rows, up_matrix, preferred_element_type=jnp.float32)
    gate = gate_base + delta.astype(jnp.float32)
    return (jax.nn.silu(gate) * up).astype(jnp.bfloat16)


def solution(mesh):
    in_specs = (
        P(("groups", "dp"), None),
        P(("groups", "dp"), None),
        P(),
        P(None, "dp"),
        P(None, "dp"),
        P("dp", None, None),
        P("dp", None, None),
    )
    out_specs = P("groups", "dp")
    return jax.shard_map(shards, mesh=mesh, in_specs=in_specs, out_specs=out_specs, check_vma=False)
```

profile of v0, /device:TPU:0, one launch (start us, length us, event | category | flops | bytes accessed | tf_op | source)
XLA Modules:
  0.0 414.2 jit_solution(11050166446843354838)
XLA Ops:
  6.5 29.0 %copy.20 = bf16[1,64,28672]{1,0,2:T(2,128)(2,1)} copy(bf16[1,64,28672]{2,1,0:T(8,128)(2,1)} %param.13) | data formatting | bytes 7340032 | tf_op args[6]
  35.6 0.5 broadcast.135
  36.1 157.1 %reduce = bf16[28672,64]{1,0:T(8,128)(2,1)} reduce(bf16[28672,1,64]{2,1,0:T(2,128)(2,1)} %bitcast.32, bf16[]{:T(256)} %broadcast.135), dimensions={1}, to_apply=%bitcast.23.reduce_sub_computation | reduce | bytes 7340034
  193.2 13.3 %reshape.134 = bf16[16,2,57344]{2,1,0:T(2,128)(2,1)} reshape(bf16[28672,64]{1,0:T(8,128)(2,1)} %reduce) | data formatting | bytes 7340032
  206.5 7.5 %all-to-all-start = ((bf16[16,2,57344]{2,1,0:T(2,128)(2,1)}), bf16[16,2,57344]{2,1,0:T(2,128)(2,1)}, u32[]{:S(2)}, u32[]{:S(2)}) async-start(bf16[16,2,57344]{2,1,0:T(2,128)(2,1)} %reshape.134), calls=%async_computation | async-start | bytes 7340032 | tf_op jit(solution)/shard_map/all_to_all | solution.py:39
  214.1 0.7 all-gather.2.cloned.1.call-update
  214.8 0.6 dynamic-slice
  216.1 93.4 %all-reduce = s32[128]{0:T(128)S(1)} all-reduce(s32[128]{0:T(128)S(1)} %bitcast_dynamic-update-slice_fusion), channel_id=1, replica_groups=mesh['groups'=2,'dp'=16] {'dp'}, use_global_device_ids=true, to_apply=%add | all-reduce | flops 128 | bytes 1024
  309.6 0.2 select_reduce_fusion.1
  309.9 0.2 reduce_window_sum.11
  310.1 0.2 select_reduce_fusion
  310.5 3.2 gather_fusion
  313.8 0.5 convolution_convert_fusion.1
  314.2 19.9 %all_gather.11 = bf16[512,64]{1,0:T(8,128)(2,1)S(1)} all-gather(bf16[32,64]{1,0:T(8,128)(2,1)S(1)} %convolution_convert_fusion.1), channel_id=1, replica_groups=mesh['groups'=2,'dp'=16] {'dp'}, dimensions={0}, use_global_device_ids=true | all-gather | bytes 69632 | tf_op jit(solution)/shard_map/all_gather | solution.py:40
  334.1 0.7 gather_fusion.1
  335.1 14.2 %reshape.135 = bf16[28672,1,64]{2,1,0:T(2,128)(2,1)} reshape(bf16[16,2,57344]{2,1,0:T(2,128)(2,1)} %all-to-all-done) | data formatting | bytes 7340032
  349.3 28.0 %copy.21 = bf16[1,64,28672]{2,1,0:T(8,128)(2,1)} copy(bf16[1,64,28672]{1,0,2:T(2,128)(2,1)} %bitcast.33) | data formatting | bytes 7340032 | tf_op jit(solution)/shard_map/all_to_all | solution.py:39
  377.3 2.8 copy.23
  380.1 0.2 bitcast_bitcast_fusion
  380.3 1.1 copy.22
  381.5 0.7 fusion
  382.1 0.9 copy-done.2
  383.0 11.7 %convolution_add_fusion = f32[128,1792]{1,0:T(8,128)S(1)} fusion(f32[128,1792]{1,0:T(8,128)S(1)} %fusion, bf16[128,8192]{1,0:T(8,128)(2,1)S(1)} %copy-done.2, bf16[8192,1792]{1,0:T(8,128)(2,1)} %param.10), kind=kOutput, calls=%fused_computation.4 | convolution fusion | flops 3758325760 | bytes 33292288 | tf_op jit(solution)/shard_map/dot_general | solution.py:48
  394.8 12.5 %fusion.1 = bf16[128,1792]{1,0:T(8,128)(2,1)} fusion(bf16[128,8192]{1,0:T(8,128)(2,1)S(1)} %copy-done.2, bf16[8192,1792]{1,0:T(8,128)(2,1)} %param.11, f32[128,1792]{1,0:T(8,128)S(1)} %convolution_add_fusion), kind=kOutput, calls=%fused_computation.7 | convolution fusion | flops 3759472640 | bytes 32833536 | tf_op jit(solution)/shard_map/dot_general | solution.py:49
  (29 shorter events, 0.7 us)
Async XLA Ops:
  6.5 307.2 %copy-start = (bf16[1,8192,64]{1,2,0:T(8,128)(2,1)S(1)}, bf16[1,8192,64]{1,2,0:T(8,128)(2,1)}, u32[]{:S(2)}) copy-start(bf16[1,8192,64]{1,2,0:T(8,128)(2,1)} %param.12) | copy-start | bytes 3145732
  206.5 8.3 %copy-start.5 = (u32[32]{0:T(128)S(1)}, u32[32]{0:T(128)}, u32[]{:S(2)}) copy-start(u32[32]{0:T(128)} %constant.53) | copy-start | bytes 388
  206.5 9.6 %copy-start.3 = (s32[8,1]{0,1:T(1,128)S(1)}, s32[8,1]{0,1:T(1,128)}, u32[]{:S(2)}) copy-start(s32[8,1]{0,1:T(1,128)} %param.8) | copy-start | bytes 100
  206.5 103.1 %copy-start.4 = (s32[16]{0:T(128)S(1)}, s32[16]{0:T(128)}, u32[]{:S(2)}) copy-start(s32[16]{0:T(128)} %param.9) | copy-start | bytes 196
  206.5 128.6 %all-to-all-start = ((bf16[16,2,57344]{2,1,0:T(2,128)(2,1)}), bf16[16,2,57344]{2,1,0:T(2,128)(2,1)}, u32[]{:S(2)}, u32[]{:S(2)}) async-start(bf16[16,2,57344]{2,1,0:T(2,128)(2,1)} %reshape.134), calls=%async_computation | async-start | bytes 7340032 | tf_op jit(solution)/shard_map/all_to_all | solution.py:39
  214.0 96.5 %all-gather.2.cloned.1.call-start = ((), (), s32[]{:S(2)}) async-start(), calls=%async_computation.1 | async-start | bytes 2228224 | tf_op jit(solution)/shard_map/all_gather | solution.py:21
  381.4 1.6 copy-start.2
  394.8 12.6 %copy-start.1 = (bf16[1,8192,64]{1,2,0:T(8,128)(2,1)S(1)}, bf16[1,8192,64]{1,2,0:T(8,128)(2,1)}, u32[]{:S(2)}) copy-start(bf16[1,8192,64]{1,2,0:T(8,128)(2,1)} %param.12) | copy-start | bytes 3145732
Sparse Core Ops, SparseCore 0:
  217.0 74.7 all-gather.1
where the time goes:
time: 417 us; the launch traced here: 414 us
  other arithmetic  158 us (38%)
  blocking collectives  113 us (27%)
  local copies, waits for them, and re-layouts  94.9 us (23%)
  matrix products  25.4 us (6%)
  between operations  14.3 us (3%)
  starting transfers between devices  7.58 us (2%)
    unnamed x1, other arithmetic  157 us
    unnamed x1, blocking collectives  93.4 us
    unnamed x20, local copies, waits for them, and re-layouts  61.4 us
    all_to_all x3, local copies, waits for them, and re-layouts, shards(): lax.all_to_all(adapter_up_factor, 'dp', split_axis=2, concat_axis=0, tile...  29.4 us
    all_gather x1, blocking collectives, shards(): all_low = lax.all_gather(reduced_rows, 'dp', axis=0, tiled=True)  19.9 us
    dot_general x1, matrix products, shards(): up = jnp.dot(all_rows, up_matrix, preferred_element_type=jnp.float32)  12.5 us
    dot_general x1, matrix products, shards(): jnp.dot(all_rows, gate_matrix, preferred_element_type=jnp.float32)  11.7 us
  transfers between devices with their start and end apart: 2, of which 0 were waited for; matrix products, arithmetic and copies ran while one was open for 1% of the time, Pallas kernels for 0%

commit v1 on v0

--- a/solution.py
+++ b/solution.py
@@ -1,12 +1,20 @@
+import functools
+
 import jax
 import jax.numpy as jnp
 from jax import lax
+from jax.experimental import pallas as pl
+from jax.experimental.pallas import tpu as pltpu
 from jax.sharding import PartitionSpec as P
 
 CAP = 32
-
-
-def shards(
+LANES = 128
+PLANES = 4
+F32 = jnp.float32
+BF16 = jnp.bfloat16
+
+
+def general_shards(
     tokens,
     token_adapter_index,
     adapter_slot_index,
@@ -34,21 +42,230 @@
     row_list = jnp.sum(jnp.where(mine, jnp.arange(total, dtype=jnp.int32)[:, None], 0), 0)
     selected_slot = jnp.take(all_rows, row_list, axis=0)
     reduced_rows = jnp.dot(
-        selected_slot, adapter_down_factor[0], preferred_element_type=jnp.float32
-    ).astype(jnp.bfloat16)
+        selected_slot, adapter_down_factor[0], preferred_element_type=F32
+    ).astype(BF16)
     slot_pieces = lax.all_to_all(adapter_up_factor, "dp", split_axis=2, concat_axis=0, tiled=True)
     all_low = lax.all_gather(reduced_rows, "dp", axis=0, tiled=True)
     rank_width = all_low.shape[1]
     token_low = jnp.take(all_low, slots * capacity + ranks, axis=0)
-    expanded = (token_low[:, None, :] * slot_match.astype(jnp.bfloat16)[:, :, None]).reshape(
+    expanded = (token_low[:, None, :] * slot_match.astype(BF16)[:, :, None]).reshape(
         total, count * rank_width
     )
     stacked = slot_pieces.reshape(count * rank_width, slot_pieces.shape[2])
-    delta = jnp.dot(expanded, stacked, preferred_element_type=jnp.float32).astype(jnp.bfloat16)
-    gate_base = jnp.dot(all_rows, gate_matrix, preferred_element_type=jnp.float32)
-    up = jnp.dot(all_rows, up_matrix, preferred_element_type=jnp.float32)
-    gate = gate_base + delta.astype(jnp.float32)
-    return (jax.nn.silu(gate) * up).astype(jnp.bfloat16)
+    delta = jnp.dot(expanded, stacked, preferred_element_type=F32).astype(BF16)
+    gate_base = jnp.dot(all_rows, gate_matrix, preferred_element_type=F32)
+    up = jnp.dot(all_rows, up_matrix, preferred_element_type=F32)
+    gate = gate_base + delta.astype(F32)
+    return (jax.nn.silu(gate) * up).astype(BF16)
+
+
+ANY = pl.BlockSpec(memory_space=pl.ANY)
+CHUNKS = ((2, 3), (1, 0))
+
+
+def repack_kernel(width, u_ref, *refs):
+    outs, sems = refs[:-1], refs[-1]
+    half = u_ref.shape[0] // 2
+    me, y = lax.axis_index("dp"), lax.axis_index("groups")
+    z, x, c = me // 4, (me // 2) % 2, me % 2
+    copies = []
+    for k, chunk in enumerate(CHUNKS):
+        own, core, cross, both = outs[4 * k : 4 * k + 4]
+        for i, j in enumerate(chunk):
+            zz = lax.bitwise_xor(z, j)
+            for ref, xx, cc, split in (
+                (cross, 1 - x, c, True),
+                (both, 1 - x, 1 - c, True),
+                (core, x, 1 - c, False),
+                (own, x, c, False),
+            ):
+                at = pl.multiple_of(((zz * 2 + xx) * 2 + cc) * width, LANES)
+                rows = pl.ds(pl.multiple_of(y * half, half), half) if split else pl.ds(0, 2 * half)
+                copies.append(
+                    pltpu.make_async_copy(
+                        u_ref.at[rows, pl.ds(at, width)],
+                        ref.at[:, pl.ds(i * width, width)],
+                        sems.at[len(copies)],
+                    )
+                )
+    for copy in copies:
+        copy.start()
+    for copy in copies:
+        copy.wait()
+
+
+def repack(u, width):
+    rank = u.shape[0]
+    shapes = []
+    for chunk in CHUNKS:
+        n = len(chunk) * width
+        shapes += [
+            jax.ShapeDtypeStruct((rank, n), BF16),
+            jax.ShapeDtypeStruct((rank, n), BF16),
+            jax.ShapeDtypeStruct((rank // 2, n), BF16),
+            jax.ShapeDtypeStruct((rank // 2, n), BF16),
+        ]
+    return pl.pallas_call(
+        functools.partial(repack_kernel, width),
+        out_shape=shapes,
+        in_specs=[ANY],
+        out_specs=[ANY] * len(shapes),
+        scratch_shapes=[pltpu.SemaphoreType.DMA((16,))],
+        cost_estimate=pl.CostEstimate(flops=0, bytes_accessed=3 * u.size, transcendentals=0),
+        name="repack",
+    )(u)
+
+
+def delta_kernel(e_ref, *refs):
+    stacked = jnp.concatenate([ref[...] for ref in refs[:-1]], axis=0)
+    refs[-1][...] = jnp.dot(e_ref[...], stacked, preferred_element_type=F32).astype(BF16)
+
+
+def delta_rows(e, parts, place, width):
+    rows = e.shape[0]
+    step = width // 2
+    return pl.pallas_call(
+        delta_kernel,
+        out_shape=jax.ShapeDtypeStruct((rows, width), BF16),
+        grid=(2,),
+        in_specs=[pl.BlockSpec(e.shape, lambda i: (0, 0))]
+        + [pl.BlockSpec((p.shape[0], step), lambda i: (0, 2 * place + i)) for p in parts],
+        out_specs=pl.BlockSpec((rows, step), lambda i: (0, i)),
+        cost_estimate=pl.CostEstimate(
+            flops=2 * rows * e.shape[1] * width, bytes_accessed=2 * width * (rows + e.shape[1]), transcendentals=0
+        ),
+        name="delta_rows",
+    )(e, *parts)
+
+
+def base_kernel(xa_ref, xb_ref, g_ref, u_ref, gate_ref, up_ref):
+    @pl.when(pl.program_id(0) == 0)
+    def _():
+        gate_ref[...] = jnp.zeros_like(gate_ref)
+        up_ref[...] = jnp.zeros_like(up_ref)
+
+    x = jnp.concatenate([xa_ref[...], xb_ref[...]], axis=0)
+    gate_ref[...] += jnp.dot(x, g_ref[...], preferred_element_type=F32)
+    up_ref[...] += jnp.dot(x, u_ref[...], preferred_element_type=F32)
+
+
+def base(xa, xb, gate_matrix, up_matrix):
+    depth, width = gate_matrix.shape
+    block = 512
+    rows = xa.shape[0]
+    x_spec = pl.BlockSpec((rows, block), lambda k: (0, k))
+    w_spec = pl.BlockSpec((block, width), lambda k: (k, 0))
+    o_spec = pl.BlockSpec((2 * rows, width), lambda k: (0, 0))
+    shape = jax.ShapeDtypeStruct((2 * rows, width), F32)
+    return pl.pallas_call(
+        base_kernel,
+        out_shape=[shape, shape],
+        grid=(depth // block,),
+        in_specs=[x_spec, x_spec, w_spec, w_spec],
+        out_specs=[o_spec, o_spec],
+        compiler_params=pltpu.CompilerParams(vmem_limit_bytes=40 * 1024 * 1024),
+        cost_estimate=pl.CostEstimate(
+            flops=8 * rows * depth * width, bytes_accessed=4 * depth * width, transcendentals=0
+        ),
+        name="base",
+    )(xa, xb, gate_matrix, up_matrix)
+
+
+def finish_kernel(gate_ref, up_ref, pick_ref, order_ref, *refs):
+    stacked = jnp.concatenate([ref[...] for ref in refs[:-1]], axis=0)
+    delta = jnp.dot(pick_ref[...], stacked, preferred_element_type=F32)
+    gate = gate_ref[...] + delta
+    hidden = (gate / (1.0 + jnp.exp(-gate)) * up_ref[...]).astype(BF16)
+    refs[-1][...] = jnp.dot(order_ref[...], hidden, preferred_element_type=F32).astype(BF16)
+
+
+def finish(gate, up, pick, order, rows_by_plane):
+    total, width = gate.shape
+    step = width // 7 if width % (7 * LANES) == 0 else width
+    col = lambda a: pl.BlockSpec((a.shape[0], step), lambda i: (0, i))
+    whole = lambda a: pl.BlockSpec(a.shape, lambda i: (0, 0))
+    return pl.pallas_call(
+        finish_kernel,
+        out_shape=jax.ShapeDtypeStruct((total, width), BF16),
+        grid=(width // step,),
+        in_specs=[col(gate), col(up), whole(pick), whole(order)] + [col(r) for r in rows_by_plane],
+        out_specs=pl.BlockSpec((total, step), lambda i: (0, i)),
+        cost_estimate=pl.CostEstimate(flops=0, bytes_accessed=4 * total * width * 4, transcendentals=total * width),
+        name="finish",
+    )(gate, up, pick, order, *rows_by_plane)
+
+
+def plane_shards(
+    tokens,
+    token_adapter_index,
+    adapter_slot_index,
+    gate_matrix,
+    up_matrix,
+    adapter_down_factor,
+    adapter_up_factor,
+):
+    count = lax.axis_size("dp")
+    me, y = lax.axis_index("dp"), lax.axis_index("groups")
+    z = me // 4
+    own_rows, depth = tokens.shape
+    total = own_rows * count
+    width = gate_matrix.shape[1]
+    rank = adapter_up_factor.shape[1]
+
+    def swap(value, k):
+        return lax.ppermute(value, "dp", [(d, d ^ k) for d in range(count)])
+
+    def other(value):
+        return lax.ppermute(value, "groups", [(0, 1), (1, 0)])
+
+    ids = jnp.broadcast_to(token_adapter_index.astype(BF16), (own_rows, LANES))
+    packed = jnp.concatenate([tokens, ids], axis=1)
+    by_plane = [packed] + [swap(packed, 4 * j) for j in range(1, PLANES)]
+    near = jnp.concatenate([p for q in by_plane for p in (q, swap(q, 2))], axis=0)
+    far = swap(near, 1)
+
+    pieces = repack(adapter_up_factor[0], width)
+    stacks = []
+    for k in range(len(CHUNKS)):
+        own, core, cross, both = pieces[4 * k : 4 * k + 4]
+        core = swap(core, 1)
+        cross, both = swap(cross, 2), swap(both, 3)
+        stacks.append((own, core, cross, other(cross), both, other(both)))
+
+    place = jnp.arange(total, dtype=jnp.int32)
+    block = place // own_rows
+    distance = (block % 8) * 2 + block // 8
+    order_of = (distance ^ me) * own_rows + place % own_rows
+    all_ids = jnp.concatenate([near[:, depth], far[:, depth]]).astype(jnp.int32)
+    adapters = jnp.arange(count, dtype=jnp.int32)
+    slots = jnp.sum(jnp.where(all_ids[:, None] == adapters[None, :], adapter_slot_index[None, :], 0), 1)
+    planes = slots // 4
+    before = (planes[None, :] == planes[:, None]) & (order_of[None, :] < order_of[:, None])
+    ranks = jnp.sum(before.astype(jnp.int32), 1)
+
+    low = jnp.concatenate(
+        [jnp.dot(v[:, :depth], adapter_down_factor[0], preferred_element_type=F32) for v in (near, far)], axis=0
+    ).astype(BF16)
+    mine = (slots == me)[None, :] & (ranks[None, :] == place[:, None])
+    low = jnp.dot(mine.astype(BF16), low, preferred_element_type=F32).astype(BF16)
+
+    def turned(v):
+        return jnp.where(y == 0, v, jnp.concatenate([v[:, rank // 2 :], v[:, : rank // 2]], axis=1))
+
+    e = jnp.concatenate([low, swap(low, 1), turned(swap(low, 2)), turned(swap(low, 3))], axis=1)
+
+    rows_by_plane = {}
+    for chunk, parts in zip(CHUNKS, stacks):
+        for i, j in enumerate(chunk):
+            out = delta_rows(e, parts, i, width)
+            rows_by_plane[j] = swap(out, 4 * j) if j else out
+    rows_by_plane = [rows_by_plane[j] for j in range(PLANES)]
+
+    gate, up = base(near, far, gate_matrix, up_matrix)
+    at = (planes ^ z) * total + ranks
+    pick = (at[:, None] == jnp.arange(PLANES * total, dtype=jnp.int32)[None, :]).astype(BF16)
+    order = (order_of[None, :] == place[:, None]).astype(BF16)
+    return finish(gate, up, pick, order, rows_by_plane)
 
 
 def solution(mesh):
@@ -62,4 +279,5 @@
         P("dp", None, None),
     )
     out_specs = P("groups", "dp")
+    shards = plane_shards if mesh.shape["dp"] == 16 and mesh.shape["groups"] == 2 else general_shards
     return jax.shard_map(shards, mesh=mesh, in_specs=in_specs, out_specs=out_specs, check_vma=False)

time: 417 us -> 222 us (0.53)
  the two profiles are of different devices: /device:TPU:0 before, /device:TPU:18 now
where the time goes in v1:
time: 222 us
  Pallas kernels  126 us (57%)
  waiting for transfers between devices  62.2 us (28%)
  starting transfers between devices  23.5 us (11%)
  local copies, waits for them, and re-layouts  4.65 us (2%)
  other arithmetic  4.32 us (2%)
    pallas_call x1, Pallas kernels, repack(): pl.pallas_call(functools.partial(repack_kernel, width), out_shape=shapes,...  84.7 us
    ppermute x20, waiting for transfers between devices, swap(): return lax.ppermute(value, 'dp', [(d, d ^ k) for d in range(count)])  53.3 us
    pallas_call x1, Pallas kernels, base(): pl.pallas_call(base_kernel, out_shape=[shape, shape], grid=(depth // bloc...  24.8 us
    ppermute x20, starting transfers between devices, swap(): return lax.ppermute(value, 'dp', [(d, d ^ k) for d in range(count)])  18.4 us
    pallas_call x4, Pallas kernels, delta_rows(): pl.pallas_call(delta_kernel, out_shape=jax.ShapeDtypeStruct((rows, width)...  9.56 us
    ppermute x4, waiting for transfers between devices, other(): return lax.ppermute(value, 'groups', [(0, 1), (1, 0)])  8.87 us
    pallas_call x1, Pallas kernels, finish(): pl.pallas_call(finish_kernel, out_shape=jax.ShapeDtypeStruct((total, widt...  6.72 us
    ppermute x4, starting transfers between devices, other(): return lax.ppermute(value, 'groups', [(0, 1), (1, 0)])  5.13 us
  transfers between devices with their start and end apart: 24, of which 12 were waited for; matrix products, arithmetic and copies ran while one was open for 2% of the time, Pallas kernels for 54%

profile of v1, /device:TPU:18, one launch (start us, length us, event | category | flops | bytes accessed | tf_op | source)
XLA Modules:
  0.0 221.6 jit_solution(16439206699686224340)
XLA Ops:
  1.8 1.6 collective-permute-start.1
  4.3 1.6 collective-permute-start.5
  5.8 2.4 %collective-permute-done.1 = bf16[8,8320]{1,0:T(8,128)(2,1)S(1)} collective-permute-done((bf16[8,8320]{1,0:T(8,128)(2,1)S(1)}, bf16[8,8320]{1,0:T(8,128)(2,1)S(1)}, u32[]{:S(2)}, u32[]{:S(2)}) %collective-permute-start.1) | collective-permute-done | bytes 133152 | tf_op jit(solution)/shard_map/ppermute | solution.py:216
  8.8 4.9 %collective-permute-done.3 = bf16[8,8320]{1,0:T(8,128)(2,1)S(1)} collective-permute-done((bf16[8,8320]{1,0:T(8,128)(2,1)S(1)}, bf16[8,8320]{1,0:T(8,128)(2,1)S(1)}, u32[]{:S(2)}, u32[]{:S(2)}) %collective-permute-start.3) | collective-permute-done | bytes 133152 | tf_op jit(solution)/shard_map/ppermute | solution.py:216
  14.8 2.4 %collective-permute-done.5 = bf16[8,8320]{1,0:T(8,128)(2,1)S(1)} collective-permute-done((bf16[8,8320]{1,0:T(8,128)(2,1)S(1)}, bf16[8,8320]{1,0:T(8,128)(2,1)S(1)}, u32[]{:S(2)}, u32[]{:S(2)}) %collective-permute-start.5) | collective-permute-done | bytes 133152 | tf_op jit(solution)/shard_map/ppermute | solution.py:216
  18.9 3.2 %collective-permute-done.6 = bf16[8,8320]{1,0:T(8,128)(2,1)S(1)} collective-permute-done((bf16[8,8320]{1,0:T(8,128)(2,1)S(1)}, bf16[8,8320]{1,0:T(8,128)(2,1)S(1)}, u32[]{:S(2)}, u32[]{:S(2)}) %collective-permute-start.6) | collective-permute-done | bytes 133152 | tf_op jit(solution)/shard_map/ppermute | solution.py:216
  22.2 84.7 %repack.1 = (bf16[64,3584]{1,0:T(8,128)(2,1)}, bf16[64,3584]{1,0:T(8,128)(2,1)}, bf16[32,3584]{1,0:T(8,128)(2,1)}, bf16[32,3584]{1,0:T(8,128)(2,1)}, bf16[64,358...) custom-call(bf16[64,28672]{1,0:T(8,128)(2,1)} %bitcast.8), custom_call_target="tpu_custom_call" | custom-call | bytes 5505024 | tf_op jit(solution)/shard_map/repack/pallas_call | solution.py:108
  113.3 24.8 %base.1 = (f32[128,1792]{1,0:T(8,128)S(1)}, f32[128,1792]{1,0:T(8,128)S(1)}) custom-call(bf16[64,8320]{1,0:T(8,128)(2,1)S(1)} %constant_dynamic-update-slice_fusion.xa_ref, bf16[64,8320]{1,0:T(8,128)(2,1)S(1)} %collective-permute-done.7.xb_ref, bf16[8192,1792]{1,0:T(8,128)(2,1)} %g_ref.1, bf16[8192,1792]{1,0:T(8,128)(2,1)} %u_ref.1), custom_call_target="tpu_custom_call" | custom-call | flops 7516192768 | bytes 58720256 | tf_op jit(solution)/shard_map/base/pallas_call | solution.py:160
  141.6 2.3 %collective-permute-done.9 = bf16[128,64]{1,0:T(8,128)(2,1)S(1)} collective-permute-done((bf16[128,64]{1,0:T(8,128)(2,1)S(1)}, bf16[128,64]{1,0:T(8,128)(2,1)S(1)}, u32[]{:S(2)}, u32[]{:S(2)}) %collective-permute-start.9) | collective-permute-done | bytes 16416 | tf_op jit(solution)/shard_map/ppermute | solution.py:216
  144.0 1.7 collective-permute-start.17
  145.9 1.6 collective-permute-start.13
  147.5 4.3 %collective-permute-done.20.refs_4_ = bf16[32,3584]{1,0:T(8,128)(2,1)S(1)} collective-permute-done((bf16[32,3584]{1,0:T(8,128)(2,1)S(1)}, bf16[32,3584]{1,0:T(8,128)(2,1)S(1)}, u32[]{:S(2)}, u32[]{:S(2)}) %collective-permute-start.20) | collective-permute-done | bytes 229408 | tf_op jit(solution)/shard_map/ppermute | solution.py:216
  151.8 1.5 collective-permute-start.15
  153.8 1.5 collective-permute-start.21
  156.1 4.3 %collective-permute-done.15.refs_5_ = bf16[32,3584]{1,0:T(8,128)(2,1)S(1)} collective-permute-done((bf16[32,3584]{1,0:T(8,128)(2,1)}, bf16[32,3584]{1,0:T(8,128)(2,1)S(1)}, u32[]{:S(2)}, u32[]{:S(2)}) %collective-permute-start.15) | collective-permute-done | bytes 229408 | tf_op jit(solution)/shard_map/ppermute | solution.py:219
  161.1 2.4 %delta_rows.5 = bf16[128,1792]{1,0:T(8,128)(2,1)} custom-call(bf16[128,256]{1,0:T(8,128)(2,1)} %pad_maximum_fusion.1.e_ref, bf16[64,3584]{1,0:T(8,128)(2,1)} %get-tuple-element.17.refs_0_, bf16[64,3584]{1,0:T(8,128)(2,1)} %collective-permute-done.11.refs_1_, bf16[32,3584]{1,0:T(8,128)(2,1)} %copy-done.5, bf16[32,3584]{1,0:T(8,128)(2,1)} %copy-done.7, ...), custom_call_target="tpu_custom_call" | custom-call | flops 117440512 | bytes 1376256 | tf_op jit(solution)/shard_map/delta_rows/pallas_call | solution.py:127
  165.3 4.1 %collective-permute-done.21.refs_5_ = bf16[32,3584]{1,0:T(8,128)(2,1)S(1)} collective-permute-done((bf16[32,3584]{1,0:T(8,128)(2,1)S(1)}, bf16[32,3584]{1,0:T(8,128)(2,1)S(1)}, u32[]{:S(2)}, u32[]{:S(2)}) %collective-permute-start.21) | collective-permute-done | bytes 229408 | tf_op jit(solution)/shard_map/ppermute | solution.py:219
  170.2 2.4 %delta_rows.6 = bf16[128,1792]{1,0:T(8,128)(2,1)} custom-call(bf16[128,256]{1,0:T(8,128)(2,1)} %pad_maximum_fusion.1.e_ref, bf16[64,3584]{1,0:T(8,128)(2,1)} %get-tuple-element.21.refs_0_, bf16[64,3584]{1,0:T(8,128)(2,1)} %copy-done.4, bf16[32,3584]{1,0:T(8,128)(2,1)} %collective-permute-done.18.refs_2_, bf16[32,3584]{1,0:T(8,128)(2,1)} %copy-done.9, ...), custom_call_target="tpu_custom_call" | custom-call | flops 117440512 | bytes 1376256 | tf_op jit(solution)/shard_map/delta_rows/pallas_call | solution.py:127
  173.3 2.4 %delta_rows.7 = bf16[128,1792]{1,0:T(8,128)(2,1)} custom-call(bf16[128,256]{1,0:T(8,128)(2,1)} %pad_maximum_fusion.1.e_ref, bf16[64,3584]{1,0:T(8,128)(2,1)} %get-tuple-element.21.refs_0_, bf16[64,3584]{1,0:T(8,128)(2,1)} %copy-done.4, bf16[32,3584]{1,0:T(8,128)(2,1)} %collective-permute-done.18.refs_2_, bf16[32,3584]{1,0:T(8,128)(2,1)} %copy-done.9, ...), custom_call_target="tpu_custom_call" | custom-call | flops 117440512 | bytes 1376256 | tf_op jit(solution)/shard_map/delta_rows/pallas_call | solution.py:127
  175.7 1.7 collective-permute-start.23
  178.1 2.4 %delta_rows.4.refs_0_ = bf16[128,1792]{1,0:T(8,128)(2,1)} custom-call(bf16[128,256]{1,0:T(8,128)(2,1)} %pad_maximum_fusion.1.e_ref, bf16[64,3584]{1,0:T(8,128)(2,1)} %get-tuple-element.17.refs_0_, bf16[64,3584]{1,0:T(8,128)(2,1)} %collective-permute-done.11.refs_1_, bf16[32,3584]{1,0:T(8,128)(2,1)} %copy-done.5, bf16[32,3584]{1,0:T(8,128)(2,1)} %copy-done.7, ...), custom_call_target="tpu_custom_call" | custom-call | flops 117440512 | bytes 1376256 | tf_op jit(solution)/shard_map/delta_rows/pallas_call | solution.py:127
  180.5 23.0 %collective-permute-done.22.refs_2_ = bf16[128,1792]{1,0:T(8,128)(2,1)S(1)} collective-permute-done((bf16[128,1792]{1,0:T(8,128)(2,1)}, bf16[128,1792]{1,0:T(8,128)(2,1)S(1)}, u32[]{:S(2)}, u32[]{:S(2)}) %collective-permute-start.22) | collective-permute-done | bytes 458784 | tf_op jit(solution)/shard_map/ppermute | solution.py:216
  203.5 10.6 %collective-permute-done.23.refs_3_ = bf16[128,1792]{1,0:T(8,128)(2,1)S(1)} collective-permute-done((bf16[128,1792]{1,0:T(8,128)(2,1)}, bf16[128,1792]{1,0:T(8,128)(2,1)S(1)}, u32[]{:S(2)}, u32[]{:S(2)}) %collective-permute-start.23) | collective-permute-done | bytes 458784 | tf_op jit(solution)/shard_map/ppermute | solution.py:216
  214.9 6.7 %finish.1 = bf16[128,1792]{1,0:T(8,128)(2,1)} custom-call(f32[128,1792]{1,0:T(8,128)} %copy-done.2, f32[128,1792]{1,0:T(8,128)} %copy-done.3, bf16[128,512]{1,0:T(8,128)(2,1)} %fusion.4.pick_ref, bf16[128,128]{1,0:T(8,128)(2,1)} %fusion.5.order_ref, bf16[128,1792]{1,0:T(8,128)(2,1)} %delta_rows.4.refs_0_, bf16[128,1792]{1,0:T(8,128)(2,1)} %copy-done.11, ...), custom_call_target="tpu_custom_call" | custom-call | bytes 3670016 | tf_op jit(solution)/shard_map/finish/pallas_call | solution.py:187
  (92 shorter events, 23.0 us)
Async XLA Ops:
  1.8 6.5 %collective-permute-start.1 = (bf16[8,8320]{1,0:T(8,128)(2,1)S(1)}, bf16[8,8320]{1,0:T(8,128)(2,1)S(1)}, u32[]{:S(2)}, u32[]{:S(2)}) collective-permute-start(bf16[8,8320]{1,0:T(8,128)(2,1)S(1)} %get-tuple-element.25), channel_id=1, source_target_pairs={{0,4},{1,5},{2,6},{3,7},{4,0},{5,1},{6,2},{7,3},{8,12},{9,13},{10,... | collective-permute-start | bytes 399368 | tf_op jit(solution)/shard_map/ppermute | solution.py:216
  3.4 5.4 %collective-permute-start = (bf16[8,8320]{1,0:T(8,128)(2,1)S(1)}, bf16[8,8320]{1,0:T(8,128)(2,1)S(1)}, u32[]{:S(2)}, u32[]{:S(2)}) collective-permute-start(bf16[8,8320]{1,0:T(8,128)(2,1)S(1)} %get-tuple-element.25), channel_id=1, source_target_pairs={{0,2},{1,3},{2,0},{3,1},{4,6},{5,7},{6,4},{7,5},{8,10},{9,11},{10,... | collective-permute-start | bytes 399368 | tf_op jit(solution)/shard_map/ppermute | solution.py:216
  3.9 9.8 %collective-permute-start.3 = (bf16[8,8320]{1,0:T(8,128)(2,1)S(1)}, bf16[8,8320]{1,0:T(8,128)(2,1)S(1)}, u32[]{:S(2)}, u32[]{:S(2)}) collective-permute-start(bf16[8,8320]{1,0:T(8,128)(2,1)S(1)} %get-tuple-element.25), channel_id=1, source_target_pairs={{0,8},{1,9},{2,10},{3,11},{4,12},{5,13},{6,14},{7,15},{8,0},{9,1},... | collective-permute-start | bytes 399368 | tf_op jit(solution)/shard_map/ppermute | solution.py:216
  4.3 12.9 %collective-permute-start.5 = (bf16[8,8320]{1,0:T(8,128)(2,1)S(1)}, bf16[8,8320]{1,0:T(8,128)(2,1)S(1)}, u32[]{:S(2)}, u32[]{:S(2)}) collective-permute-start(bf16[8,8320]{1,0:T(8,128)(2,1)S(1)} %get-tuple-element.25), channel_id=1, source_target_pairs={{0,12},{1,13},{2,14},{3,15},{4,8},{5,9},{6,10},{7,11},{8,4},{9,5},... | collective-permute-start | bytes 399368 | tf_op jit(solution)/shard_map/ppermute | solution.py:216
  8.2 10.4 %collective-permute-start.2 = (bf16[8,8320]{1,0:T(8,128)(2,1)S(1)}, bf16[8,8320]{1,0:T(8,128)(2,1)S(1)}, u32[]{:S(2)}, u32[]{:S(2)}) collective-permute-start(bf16[8,8320]{1,0:T(8,128)(2,1)S(1)} %collective-permute-done.1), channel_id=1, source_target_pairs={{0,2},{1,3},{2,0},{3,1},{4,6},{5,7},{6,4},{7,5},{8,10},{9,11},{10,... | collective-permute-start | bytes 399368 | tf_op jit(solution)/shard_map/ppermute | solution.py:216
  13.7 5.2 %collective-permute-start.4 = (bf16[8,8320]{1,0:T(8,128)(2,1)S(1)}, bf16[8,8320]{1,0:T(8,128)(2,1)S(1)}, u32[]{:S(2)}, u32[]{:S(2)}) collective-permute-start(bf16[8,8320]{1,0:T(8,128)(2,1)S(1)} %collective-permute-done.3), channel_id=1, source_target_pairs={{0,2},{1,3},{2,0},{3,1},{4,6},{5,7},{6,4},{7,5},{8,10},{9,11},{10,... | collective-permute-start | bytes 399368 | tf_op jit(solution)/shard_map/ppermute | solution.py:216
  17.1 5.0 %collective-permute-start.6 = (bf16[8,8320]{1,0:T(8,128)(2,1)S(1)}, bf16[8,8320]{1,0:T(8,128)(2,1)S(1)}, u32[]{:S(2)}, u32[]{:S(2)}) collective-permute-start(bf16[8,8320]{1,0:T(8,128)(2,1)S(1)} %collective-permute-done.5), channel_id=1, source_target_pairs={{0,2},{1,3},{2,0},{3,1},{4,6},{5,7},{6,4},{7,5},{8,10},{9,11},{10,... | collective-permute-start | bytes 399368 | tf_op jit(solution)/shard_map/ppermute | solution.py:216
  22.1 89.4 %collective-permute-start.7 = (bf16[64,8320]{1,0:T(8,128)(2,1)S(1)}, bf16[64,8320]{1,0:T(8,128)(2,1)S(1)}, u32[]{:S(2)}, u32[]{:S(2)}) collective-permute-start(bf16[64,8320]{1,0:T(8,128)(2,1)S(1)} %constant_dynamic-update-slice_fusion.xa_ref), channel_id=1, source_target_pairs={{0,1},{1,0},{2,3},{3,2},{4,5},{5,4},{6,7},{7,6},{8,9},{9,8},{10,11... | collective-permute-start | bytes 3194888 | tf_op jit(solution)/shard_map/ppermute | solution.py:216
  106.9 46.4 %collective-permute-start.11 = (bf16[64,3584]{1,0:T(8,128)(2,1)}, bf16[64,3584]{1,0:T(8,128)(2,1)}, u32[]{:S(2)}, u32[]{:S(2)}) collective-permute-start(bf16[64,3584]{1,0:T(8,128)(2,1)} %get-tuple-element.18), channel_id=1, source_target_pairs={{0,1},{1,0},{2,3},{3,2},{4,5},{5,4},{6,7},{7,6},{8,9},{9,8},{10,11... | collective-permute-start | bytes 1376264 | tf_op jit(solution)/shard_map/ppermute | solution.py:216
  107.4 36.6 %collective-permute-start.12 = (bf16[32,3584]{1,0:T(8,128)(2,1)}, bf16[32,3584]{1,0:T(8,128)(2,1)S(1)}, u32[]{:S(2)}, u32[]{:S(2)}) collective-permute-start(bf16[32,3584]{1,0:T(8,128)(2,1)} %get-tuple-element.19), channel_id=1, source_target_pairs={{0,2},{1,3},{2,0},{3,1},{4,6},{5,7},{6,4},{7,5},{8,10},{9,11},{10,... | collective-permute-start | bytes 688136 | tf_op jit(solution)/shard_map/ppermute | solution.py:216
  108.9 36.8 %collective-permute-start.14 = (bf16[32,3584]{1,0:T(8,128)(2,1)}, bf16[32,3584]{1,0:T(8,128)(2,1)}, u32[]{:S(2)}, u32[]{:S(2)}) collective-permute-start(bf16[32,3584]{1,0:T(8,128)(2,1)} %get-tuple-element.20), channel_id=1, source_target_pairs={{0,3},{1,2},{2,1},{3,0},{4,7},{5,6},{6,5},{7,4},{8,11},{9,10},{10,... | collective-permute-start | bytes 688136 | tf_op jit(solution)/shard_map/ppermute | solution.py:216
  108.9 37.0 %collective-permute-start.18 = (bf16[32,3584]{1,0:T(8,128)(2,1)}, bf16[32,3584]{1,0:T(8,128)(2,1)}, u32[]{:S(2)}, u32[]{:S(2)}) collective-permute-start(bf16[32,3584]{1,0:T(8,128)(2,1)} %get-tuple-element.23), channel_id=1, source_target_pairs={{0,2},{1,3},{2,0},{3,1},{4,6},{5,7},{6,4},{7,5},{8,10},{9,11},{10,... | collective-permute-start | bytes 688136 | tf_op jit(solution)/shard_map/ppermute | solution.py:216
  112.7 27.3 %collective-permute-start.10 = (bf16[128,64]{1,0:T(8,128)(2,1)S(1)}, bf16[128,64]{1,0:T(8,128)(2,1)S(1)}, u32[]{:S(2)}, u32[]{:S(2)}) collective-permute-start(bf16[128,64]{1,0:T(8,128)(2,1)S(1)} %convolution_convert_fusion), channel_id=1, source_target_pairs={{0,3},{1,2},{2,1},{3,0},{4,7},{5,6},{6,5},{7,4},{8,11},{9,10},{10,... | collective-permute-start | bytes 49160 | tf_op jit(solution)/shard_map/ppermute | solution.py:216
  140.0 3.9 %collective-permute-start.9 = (bf16[128,64]{1,0:T(8,128)(2,1)S(1)}, bf16[128,64]{1,0:T(8,128)(2,1)S(1)}, u32[]{:S(2)}, u32[]{:S(2)}) collective-permute-start(bf16[128,64]{1,0:T(8,128)(2,1)S(1)} %convolution_convert_fusion), channel_id=1, source_target_pairs={{0,2},{1,3},{2,0},{3,1},{4,6},{5,7},{6,4},{7,5},{8,10},{9,11},{10,... | collective-permute-start | bytes 49160 | tf_op jit(solution)/shard_map/ppermute | solution.py:216
  143.9 7.9 %collective-permute-start.20 = (bf16[32,3584]{1,0:T(8,128)(2,1)S(1)}, bf16[32,3584]{1,0:T(8,128)(2,1)S(1)}, u32[]{:S(2)}, u32[]{:S(2)}) collective-permute-start(bf16[32,3584]{1,0:T(8,128)(2,1)S(1)} %copy-done.14), channel_id=1, source_target_pairs={{0,3},{1,2},{2,1},{3,0},{4,7},{5,6},{6,5},{7,4},{8,11},{9,10},{10,... | collective-permute-start | bytes 688136 | tf_op jit(solution)/shard_map/ppermute | solution.py:216
  144.0 20.9 %collective-permute-start.17 = (bf16[64,3584]{1,0:T(8,128)(2,1)}, bf16[64,3584]{1,0:T(8,128)(2,1)S(1)}, u32[]{:S(2)}, u32[]{:S(2)}) collective-permute-start(bf16[64,3584]{1,0:T(8,128)(2,1)} %get-tuple-element.22), channel_id=1, source_target_pairs={{0,1},{1,0},{2,3},{3,2},{4,5},{5,4},{6,7},{7,6},{8,9},{9,8},{10,11... | collective-permute-start | bytes 1376264 | tf_op jit(solution)/shard_map/ppermute | solution.py:216
  145.7 8.1 %collective-permute-start.8 = (bf16[128,64]{1,0:T(8,128)(2,1)S(1)}, bf16[128,64]{1,0:T(8,128)(2,1)S(1)}, u32[]{:S(2)}, u32[]{:S(2)}) collective-permute-start(bf16[128,64]{1,0:T(8,128)(2,1)S(1)} %convolution_convert_fusion), channel_id=1, source_target_pairs={{0,1},{1,0},{2,3},{3,2},{4,5},{5,4},{6,7},{7,6},{8,9},{9,8},{10,11... | collective-permute-start | bytes 49160 | tf_op jit(solution)/shard_map/ppermute | solution.py:216
  145.9 10.3 %collective-permute-start.13 = (bf16[32,3584]{1,0:T(8,128)(2,1)S(1)}, bf16[32,3584]{1,0:T(8,128)(2,1)S(1)}, u32[]{:S(2)}, u32[]{:S(2)}) collective-permute-start(bf16[32,3584]{1,0:T(8,128)(2,1)S(1)} %collective-permute-done.12.refs_2_), channel_id=1, source_target_pairs={{0,16},{16,0},{1,17},{17,1},{2,18},{18,2},{3,19},{19,3},{4,20},{20... | collective-permute-start | bytes 688136 | tf_op jit(solution)/shard_map/ppermute | solution.py:219
  151.8 8.7 %collective-permute-start.15 = (bf16[32,3584]{1,0:T(8,128)(2,1)}, bf16[32,3584]{1,0:T(8,128)(2,1)S(1)}, u32[]{:S(2)}, u32[]{:S(2)}) collective-permute-start(bf16[32,3584]{1,0:T(8,128)(2,1)} %collective-permute-done.14.refs_4_), channel_id=1, source_target_pairs={{0,16},{16,0},{1,17},{17,1},{2,18},{18,2},{3,19},{19,3},{4,20},{20... | collective-permute-start | bytes 688136 | tf_op jit(solution)/shard_map/ppermute | solution.py:219
  153.3 12.1 %collective-permute-start.19 = (bf16[32,3584]{1,0:T(8,128)(2,1)}, bf16[32,3584]{1,0:T(8,128)(2,1)S(1)}, u32[]{:S(2)}, u32[]{:S(2)}) collective-permute-start(bf16[32,3584]{1,0:T(8,128)(2,1)} %collective-permute-done.18.refs_2_), channel_id=1, source_target_pairs={{0,16},{16,0},{1,17},{17,1},{2,18},{18,2},{3,19},{19,3},{4,20},{20... | collective-permute-start | bytes 688136 | tf_op jit(solution)/shard_map/ppermute | solution.py:219
  153.8 15.7 %collective-permute-start.21 = (bf16[32,3584]{1,0:T(8,128)(2,1)S(1)}, bf16[32,3584]{1,0:T(8,128)(2,1)S(1)}, u32[]{:S(2)}, u32[]{:S(2)}) collective-permute-start(bf16[32,3584]{1,0:T(8,128)(2,1)S(1)} %collective-permute-done.20.refs_4_), channel_id=1, source_target_pairs={{0,16},{16,0},{1,17},{17,1},{2,18},{18,2},{3,19},{19,3},{4,20},{20... | collective-permute-start | bytes 688136 | tf_op jit(solution)/shard_map/ppermute | solution.py:219
  163.5 17.0 %collective-permute-start.16 = (bf16[128,1792]{1,0:T(8,128)(2,1)}, bf16[128,1792]{1,0:T(8,128)(2,1)S(1)}, u32[]{:S(2)}, u32[]{:S(2)}) collective-permute-start(bf16[128,1792]{1,0:T(8,128)(2,1)} %delta_rows.5), channel_id=1, source_target_pairs={{0,4},{1,5},{2,6},{3,7},{4,0},{5,1},{6,2},{7,3},{8,12},{9,13},{10,... | collective-permute-start | bytes 1376264 | tf_op jit(solution)/shard_map/ppermute | solution.py:216
  172.6 31.0 %collective-permute-start.22 = (bf16[128,1792]{1,0:T(8,128)(2,1)}, bf16[128,1792]{1,0:T(8,128)(2,1)S(1)}, u32[]{:S(2)}, u32[]{:S(2)}) collective-permute-start(bf16[128,1792]{1,0:T(8,128)(2,1)} %delta_rows.6), channel_id=1, source_target_pairs={{0,8},{1,9},{2,10},{3,11},{4,12},{5,13},{6,14},{7,15},{8,0},{9,1},... | collective-permute-start | bytes 1376264 | tf_op jit(solution)/shard_map/ppermute | solution.py:216
  175.7 38.4 %collective-permute-start.23 = (bf16[128,1792]{1,0:T(8,128)(2,1)}, bf16[128,1792]{1,0:T(8,128)(2,1)S(1)}, u32[]{:S(2)}, u32[]{:S(2)}) collective-permute-start(bf16[128,1792]{1,0:T(8,128)(2,1)} %delta_rows.7), channel_id=1, source_target_pairs={{0,12},{1,13},{2,14},{3,15},{4,8},{5,9},{6,10},{7,11},{8,4},{9,5},... | collective-permute-start | bytes 1376264 | tf_op jit(solution)/shard_map/ppermute | solution.py:216
  (16 other events, 239.1 us)

commit v2 on v1

--- a/solution.py
+++ b/solution.py
@@ -60,38 +60,42 @@
 
 
 ANY = pl.BlockSpec(memory_space=pl.ANY)
+VMEM = pl.BlockSpec(memory_space=pltpu.VMEM)
 CHUNKS = ((2, 3), (1, 0))
+ROOM = 64
 
 
 def repack_kernel(width, u_ref, *refs):
-    outs, sems = refs[:-1], refs[-1]
+    outs, (held, in_sems, out_sems) = refs[:-3], refs[-3:]
     half = u_ref.shape[0] // 2
     me, y = lax.axis_index("dp"), lax.axis_index("groups")
     z, x, c = me // 4, (me // 2) % 2, me % 2
-    copies = []
+    ins, sends = [], []
     for k, chunk in enumerate(CHUNKS):
         own, core, cross, both = outs[4 * k : 4 * k + 4]
-        for i, j in enumerate(chunk):
-            zz = lax.bitwise_xor(z, j)
-            for ref, xx, cc, split in (
-                (cross, 1 - x, c, True),
-                (both, 1 - x, 1 - c, True),
-                (core, x, 1 - c, False),
-                (own, x, c, False),
-            ):
+        for ref, xx, cc, split in (
+            (cross, 1 - x, c, True),
+            (both, 1 - x, 1 - c, True),
+            (core, x, 1 - c, False),
+            (own, x, c, False),
+        ):
+            for i, j in enumerate(chunk):
+                zz = lax.bitwise_xor(z, j)
+                n = len(ins)
                 at = pl.multiple_of(((zz * 2 + xx) * 2 + cc) * width, LANES)
                 rows = pl.ds(pl.multiple_of(y * half, half), half) if split else pl.ds(0, 2 * half)
-                copies.append(
-                    pltpu.make_async_copy(
-                        u_ref.at[rows, pl.ds(at, width)],
-                        ref.at[:, pl.ds(i * width, width)],
-                        sems.at[len(copies)],
-                    )
+                here = held.at[pl.ds(0, half if split else 2 * half), pl.ds(n * width, width)]
+                ins.append(pltpu.make_async_copy(u_ref.at[rows, pl.ds(at, width)], here, in_sems.at[n]))
+                sends.append(
+                    pltpu.make_async_copy(here, ref.at[:, pl.ds(i * width, width)], out_sems.at[n])
                 )
-    for copy in copies:
+    for copy in ins:
         copy.start()
-    for copy in copies:
+    for copy, send in zip(ins, sends):
         copy.wait()
+        send.start()
+    for send in sends:
+        send.wait()
 
 
 def repack(u, width):
@@ -110,65 +114,116 @@
         out_shape=shapes,
         in_specs=[ANY],
         out_specs=[ANY] * len(shapes),
-        scratch_shapes=[pltpu.SemaphoreType.DMA((16,))],
+        scratch_shapes=[
+            pltpu.VMEM((rank, 16 * width), BF16),
+            pltpu.SemaphoreType.DMA((16,)),
+            pltpu.SemaphoreType.DMA((16,)),
+        ],
+        compiler_params=pltpu.CompilerParams(vmem_limit_bytes=16 * 1024 * 1024),
         cost_estimate=pl.CostEstimate(flops=0, bytes_accessed=3 * u.size, transcendentals=0),
         name="repack",
     )(u)
 
 
-def delta_kernel(e_ref, *refs):
-    stacked = jnp.concatenate([ref[...] for ref in refs[:-1]], axis=0)
-    refs[-1][...] = jnp.dot(e_ref[...], stacked, preferred_element_type=F32).astype(BF16)
-
-
-def delta_rows(e, parts, place, width):
+def delta_kernel(width, e_ref, *refs):
+    parts, outs = refs[:6], refs[6:]
+    for i, out in enumerate(outs):
+        stacked = jnp.concatenate([ref[:, i * width : (i + 1) * width] for ref in parts], axis=0)
+        out[...] = jnp.dot(e_ref[...], stacked, preferred_element_type=F32).astype(BF16)
+
+
+def delta_rows(e, parts, width):
     rows = e.shape[0]
-    step = width // 2
+    n = parts[0].shape[1] // width
     return pl.pallas_call(
-        delta_kernel,
-        out_shape=jax.ShapeDtypeStruct((rows, width), BF16),
-        grid=(2,),
-        in_specs=[pl.BlockSpec(e.shape, lambda i: (0, 0))]
-        + [pl.BlockSpec((p.shape[0], step), lambda i: (0, 2 * place + i)) for p in parts],
-        out_specs=pl.BlockSpec((rows, step), lambda i: (0, i)),
+        functools.partial(delta_kernel, width),
+        out_shape=[jax.ShapeDtypeStruct((rows, width), BF16)] * n,
+        in_specs=[VMEM] * (1 + len(parts)),
+        out_specs=[VMEM] * n,
+        compiler_params=pltpu.CompilerParams(vmem_limit_bytes=16 * 1024 * 1024),
         cost_estimate=pl.CostEstimate(
-            flops=2 * rows * e.shape[1] * width, bytes_accessed=2 * width * (rows + e.shape[1]), transcendentals=0
+            flops=2 * rows * e.shape[1] * width * n,
+            bytes_accessed=2 * n * width * (rows + e.shape[1]),
+            transcendentals=0,
         ),
         name="delta_rows",
     )(e, *parts)
 
 
-def base_kernel(xa_ref, xb_ref, g_ref, u_ref, gate_ref, up_ref):
-    @pl.when(pl.program_id(0) == 0)
-    def _():
-        gate_ref[...] = jnp.zeros_like(gate_ref)
-        up_ref[...] = jnp.zeros_like(up_ref)
-
-    x = jnp.concatenate([xa_ref[...], xb_ref[...]], axis=0)
-    gate_ref[...] += jnp.dot(x, g_ref[...], preferred_element_type=F32)
-    up_ref[...] += jnp.dot(x, u_ref[...], preferred_element_type=F32)
-
-
-def base(xa, xb, gate_matrix, up_matrix):
-    depth, width = gate_matrix.shape
-    block = 512
-    rows = xa.shape[0]
-    x_spec = pl.BlockSpec((rows, block), lambda k: (0, k))
-    w_spec = pl.BlockSpec((block, width), lambda k: (k, 0))
-    o_spec = pl.BlockSpec((2 * rows, width), lambda k: (0, 0))
-    shape = jax.ShapeDtypeStruct((2 * rows, width), F32)
+BLOCK = 512
+SLOTS = 3
+
+
+def base_kernel(first, steps, rows, more, *refs):
+    x_refs, (g_ref, u_ref), refs = refs[:4], refs[4:6], refs[6:]
+    sums, refs = (refs[:2], refs[2:]) if more else ((), refs)
+    gate_ref, up_ref, x_held, g_held, u_held, x_sems, g_sems, u_sems = refs
+
+    def weights(k, slot):
+        at = pl.ds(pl.multiple_of((first + k) * BLOCK, BLOCK), BLOCK)
+        return (
+            pltpu.make_async_copy(g_ref.at[at], g_held.at[slot], g_sems.at[slot]),
+            pltpu.make_async_copy(u_ref.at[at], u_held.at[slot], u_sems.at[slot]),
+        )
+
+    columns = pl.ds(first * BLOCK, steps * BLOCK)
+    loads = [
+        pltpu.make_async_copy(ref.at[:, columns], x_held.at[pl.ds(i * rows, rows)], x_sems.at[i])
+        for i, ref in enumerate(x_refs)
+    ]
+    for copy in loads:
+        copy.start()
+    for k in range(min(SLOTS, steps)):
+        for copy in weights(k, k):
+            copy.start()
+    gate_ref[...] = sums[0][...] if more else jnp.zeros_like(gate_ref)
+    up_ref[...] = sums[1][...] if more else jnp.zeros_like(up_ref)
+    for copy in loads:
+        copy.wait()
+
+    def step(k, carry):
+        slot = lax.rem(k, SLOTS)
+        gate_copy, up_copy = weights(k, slot)
+        x = x_held[:, pl.ds(pl.multiple_of(k * BLOCK, BLOCK), BLOCK)]
+        gate_copy.wait()
+        gate_ref[...] += jnp.dot(x, g_held[slot], preferred_element_type=F32)
+        up_copy.wait()
+        up_ref[...] += jnp.dot(x, u_held[slot], preferred_element_type=F32)
+
+        @pl.when(k + SLOTS < steps)
+        def _():
+            for copy in weights(k + SLOTS, slot):
+                copy.start()
+
+        return carry
+
+    lax.fori_loop(0, steps, step, 0)
+
+
+def base(x_parts, gate_matrix, up_matrix, first, steps, sums=()):
+    width = gate_matrix.shape[1]
+    rows = x_parts[0].shape[0]
+    total = rows * len(x_parts)
+    shape = jax.ShapeDtypeStruct((total, width), F32)
     return pl.pallas_call(
-        base_kernel,
+        functools.partial(base_kernel, first, steps, rows, bool(sums)),
         out_shape=[shape, shape],
-        grid=(depth // block,),
-        in_specs=[x_spec, x_spec, w_spec, w_spec],
-        out_specs=[o_spec, o_spec],
-        compiler_params=pltpu.CompilerParams(vmem_limit_bytes=40 * 1024 * 1024),
+        in_specs=[ANY] * (len(x_parts) + 2) + [VMEM] * len(sums),
+        out_specs=[VMEM, VMEM],
+        scratch_shapes=[
+            pltpu.VMEM((total, steps * BLOCK), BF16),
+            pltpu.VMEM((SLOTS, BLOCK, width), BF16),
+            pltpu.VMEM((SLOTS, BLOCK, width), BF16),
+            pltpu.SemaphoreType.DMA((len(x_parts),)),
+            pltpu.SemaphoreType.DMA((SLOTS,)),
+            pltpu.SemaphoreType.DMA((SLOTS,)),
+        ],
+        compiler_params=pltpu.CompilerParams(vmem_limit_bytes=32 * 1024 * 1024),
         cost_estimate=pl.CostEstimate(
-            flops=8 * rows * depth * width, bytes_accessed=4 * depth * width, transcendentals=0
+            flops=4 * total * steps * BLOCK * width, bytes_accessed=4 * steps * BLOCK * width, transcendentals=0
         ),
         name="base",
-    )(xa, xb, gate_matrix, up_matrix)
+    )(*x_parts, gate_matrix, up_matrix, *sums)
 
 
 def finish_kernel(gate_ref, up_ref, pick_ref, order_ref, *refs):
@@ -181,7 +236,7 @@
 
 def finish(gate, up, pick, order, rows_by_plane):
     total, width = gate.shape
-    step = width // 7 if width % (7 * LANES) == 0 else width
+    step = width // 2 if width % (2 * LANES) == 0 else width
     col = lambda a: pl.BlockSpec((a.shape[0], step), lambda i: (0, i))
     whole = lambda a: pl.BlockSpec(a.shape, lambda i: (0, 0))
     return pl.pallas_call(
@@ -190,6 +245,7 @@
         grid=(width // step,),
         in_specs=[col(gate), col(up), whole(pick), whole(order)] + [col(r) for r in rows_by_plane],
         out_specs=pl.BlockSpec((total, step), lambda i: (0, i)),
+        compiler_params=pltpu.CompilerParams(vmem_limit_bytes=32 * 1024 * 1024),
         cost_estimate=pl.CostEstimate(flops=0, bytes_accessed=4 * total * width * 4, transcendentals=total * width),
         name="finish",
     )(gate, up, pick, order, *rows_by_plane)
@@ -221,51 +277,79 @@
     ids = jnp.broadcast_to(token_adapter_index.astype(BF16), (own_rows, LANES))
     packed = jnp.concatenate([tokens, ids], axis=1)
     by_plane = [packed] + [swap(packed, 4 * j) for j in range(1, PLANES)]
-    near = jnp.concatenate([p for q in by_plane for p in (q, swap(q, 2))], axis=0)
-    far = swap(near, 1)
+    near = [
+        jnp.concatenate([p for q in by_plane[i : i + 2] for p in (q, swap(q, 2))], axis=0) for i in (0, 2)
+    ]
+    x_parts = (*near, *[swap(v, 1) for v in near])
 
     pieces = repack(adapter_up_factor[0], width)
     stacks = []
     for k in range(len(CHUNKS)):
         own, core, cross, both = pieces[4 * k : 4 * k + 4]
-        core = swap(core, 1)
         cross, both = swap(cross, 2), swap(both, 3)
-        stacks.append((own, core, cross, other(cross), both, other(both)))
+        stacks.append((own, swap(core, 1), cross, other(cross), both, other(both)))
 
     place = jnp.arange(total, dtype=jnp.int32)
     block = place // own_rows
     distance = (block % 8) * 2 + block // 8
     order_of = (distance ^ me) * own_rows + place % own_rows
-    all_ids = jnp.concatenate([near[:, depth], far[:, depth]]).astype(jnp.int32)
+    all_ids = jnp.concatenate([v[:, depth] for v in x_parts]).astype(jnp.int32)
     adapters = jnp.arange(count, dtype=jnp.int32)
     slots = jnp.sum(jnp.where(all_ids[:, None] == adapters[None, :], adapter_slot_index[None, :], 0), 1)
     planes = slots // 4
     before = (planes[None, :] == planes[:, None]) & (order_of[None, :] < order_of[:, None])
     ranks = jnp.sum(before.astype(jnp.int32), 1)
+    most = jnp.max(ranks)
+    all_most = jnp.maximum(most, jnp.max(other(jnp.broadcast_to(most, (8, LANES)))))
 
     low = jnp.concatenate(
-        [jnp.dot(v[:, :depth], adapter_down_factor[0], preferred_element_type=F32) for v in (near, far)], axis=0
+        [jnp.dot(v[:, :depth], adapter_down_factor[0], preferred_element_type=F32) for v in x_parts], axis=0
     ).astype(BF16)
     mine = (slots == me)[None, :] & (ranks[None, :] == place[:, None])
     low = jnp.dot(mine.astype(BF16), low, preferred_element_type=F32).astype(BF16)
+    low, x_parts = lax.optimization_barrier((low, x_parts))
 
     def turned(v):
         return jnp.where(y == 0, v, jnp.concatenate([v[:, rank // 2 :], v[:, : rank // 2]], axis=1))
 
-    e = jnp.concatenate([low, swap(low, 1), turned(swap(low, 2)), turned(swap(low, 3))], axis=1)
-
-    rows_by_plane = {}
-    for chunk, parts in zip(CHUNKS, stacks):
-        for i, j in enumerate(chunk):
-            out = delta_rows(e, parts, i, width)
-            rows_by_plane[j] = swap(out, 4 * j) if j else out
-    rows_by_plane = [rows_by_plane[j] for j in range(PLANES)]
-
-    gate, up = base(near, far, gate_matrix, up_matrix)
-    at = (planes ^ z) * total + ranks
-    pick = (at[:, None] == jnp.arange(PLANES * total, dtype=jnp.int32)[None, :]).astype(BF16)
+    lows = [low, swap(low, 1), swap(low, 2), swap(low, 3)]
+    steps = depth // BLOCK
+    early = steps // 4
+    sums = base(x_parts, gate_matrix, up_matrix, 0, early)
+    lows, sums = lax.optimization_barrier((lows, sums))
+    e = jnp.concatenate([lows[0], lows[1], turned(lows[2]), turned(lows[3])], axis=1)
+
+    def rows_of(e):
+        by_plane = {}
+        for chunk, parts in zip(CHUNKS, stacks):
+            by_plane.update(zip(chunk, delta_rows(e, parts, width)))
+        return [by_plane[j] for j in range(PLANES)]
+
+    def sent(rows):
+        return [rows[0]] + [swap(rows[j], 4 * j) for j in (1, 2, 3)]
+
+    rows, sums = lax.optimization_barrier((rows_of(e[:ROOM]), sums))
+    rows = sent(rows)
+    gate, up = base(x_parts, gate_matrix, up_matrix, early, steps - early, sums)
+
     order = (order_of[None, :] == place[:, None]).astype(BF16)
-    return finish(gate, up, pick, order, rows_by_plane)
+    plane = planes ^ z
+
+    def picked(room, start):
+        at = jnp.where((ranks >= start) & (ranks < start + room), plane * room + ranks - start, -1)
+        return (at[:, None] == jnp.arange(PLANES * room, dtype=jnp.int32)[None, :]).astype(BF16)
+
+    first = picked(ROOM, 0)
+
+    def short():
+        return finish(gate, up, first, order, rows)
+
+    def long():
+        rest = sent(rows_of(e[ROOM:]))
+        pick = jnp.concatenate([first, picked(total - ROOM, ROOM)], axis=1)
+        return finish(gate, up, pick, order, rows + rest)
+
+    return lax.cond(all_most < ROOM, short, long)
 
 
 def solution(mesh):

time: 222 us -> 108 us (0.49)
  the two profiles are of different devices: /device:TPU:18 before, /device:TPU:0 now
where the time goes in v2:
time: 108 us; the launch traced here: 107 us
  waiting for transfers between devices  36.1 us (33%)
  starting transfers between devices  26 us (24%)
  Pallas kernels  26 us (24%)
  local copies, waits for them, and re-layouts  9.3 us (9%)
  other arithmetic  6 us (6%)
  matrix products  1.76 us (2%)
  between operations  1.65 us (2%)
    ppermute x21, waiting for transfers between devices, swap(): return lax.ppermute(value, 'dp', [(d, d ^ k) for d in range(count)])  25.3 us
    pallas_call x2, Pallas kernels, base(): pl.pallas_call(functools.partial(base_kernel, first, steps, rows, bool(su...  20.7 us
    ppermute x21, starting transfers between devices, swap(): return lax.ppermute(value, 'dp', [(d, d ^ k) for d in range(count)])  19.3 us
    ppermute x5, waiting for transfers between devices, other(): return lax.ppermute(value, 'groups', [(0, 1), (1, 0)])  10.8 us
    unnamed x37, local copies, waits for them, and re-layouts  7.93 us
    ppermute x5, starting transfers between devices, other(): return lax.ppermute(value, 'groups', [(0, 1), (1, 0)])  6.65 us
  transfers between devices with their start and end apart: 26, of which 11 were waited for; matrix products, arithmetic and copies ran while one was open for 7% of the time, Pallas kernels for 23%

profile of v2, /device:TPU:0, one launch (start us, length us, event | category | flops | bytes accessed | tf_op | source)
XLA Modules:
  0.0 106.8 jit_solution(8797907762194260951)
XLA Ops:
  1.7 4.1 %collective-permute-start.6 = (bf16[8,8320]{1,0:T(8,128)(2,1)S(1)}, bf16[8,8320]{1,0:T(8,128)(2,1)S(1)}, u32[]{:S(2)}, u32[]{:S(2)}) collective-permute-start(bf16[8,8320]{1,0:T(8,128)(2,1)S(1)} %pad_maximum_fusion.2), channel_id=1, source_target_pairs={{0,8},{1,9},{2,10},{3,11},{4,12},{5,13},{6,14},{7,15},{8,0},{9,1},... | collective-permute-start | bytes 399368 | tf_op jit(solution)/shard_map/ppermute | solution.py:272
  5.8 1.3 %collective-permute-start.8 = (bf16[8,8320]{1,0:T(8,128)(2,1)S(1)}, bf16[8,8320]{1,0:T(8,128)(2,1)S(1)}, u32[]{:S(2)}, u32[]{:S(2)}) collective-permute-start(bf16[8,8320]{1,0:T(8,128)(2,1)S(1)} %pad_maximum_fusion.2), channel_id=1, source_target_pairs={{0,12},{1,13},{2,14},{3,15},{4,8},{5,9},{6,10},{7,11},{8,4},{9,5},... | collective-permute-start | bytes 399368 | tf_op jit(solution)/shard_map/ppermute | solution.py:272
  7.4 1.5 %collective-permute-start.3 = (bf16[8,8320]{1,0:T(8,128)(2,1)S(1)}, bf16[8,8320]{1,0:T(8,128)(2,1)S(1)}, u32[]{:S(2)}, u32[]{:S(2)}) collective-permute-start(bf16[8,8320]{1,0:T(8,128)(2,1)S(1)} %pad_maximum_fusion.2), channel_id=1, source_target_pairs={{0,2},{1,3},{2,0},{3,1},{4,6},{5,7},{6,4},{7,5},{8,10},{9,11},{10,... | collective-permute-start | bytes 399368 | tf_op jit(solution)/shard_map/ppermute | solution.py:272
  8.9 2.0 %copy-done.2 = bf16[1,64,28672]{2,1,0:T(8,128)(2,1)S(1)} copy-done((bf16[1,64,28672]{2,1,0:T(8,128)(2,1)S(1)}, bf16[1,64,28672]{2,1,0:T(8,128)(2,1)}, u32[]{:S(2)}) %copy-start.2) | copy-done | bytes 3670040
  11.0 2.1 %repack.1 = (bf16[64,3584]{1,0:T(8,128)(2,1)}, bf16[64,3584]{1,0:T(8,128)(2,1)S(1)}, bf16[32,3584]{1,0:T(8,128)(2,1)}, bf16[32,3584]{1,0:T(8,128)(2,1)}, bf16[64...) custom-call(bf16[64,28672]{1,0:T(8,128)(2,1)S(1)} %bitcast.12), custom_call_target="tpu_custom_call" | custom-call | bytes 5505024 | tf_op jit(solution)/shard_map/repack/pallas_call | solution.py:112
  16.0 1.8 %collective-permute-start.7 = (bf16[8,8320]{1,0:T(8,128)(2,1)S(1)}, bf16[8,8320]{1,0:T(8,128)(2,1)S(1)}, u32[]{:S(2)}, u32[]{:S(2)}) collective-permute-start(bf16[8,8320]{1,0:T(8,128)(2,1)S(1)} %collective-permute-done.6), channel_id=1, source_target_pairs={{0,2},{1,3},{2,0},{3,1},{4,6},{5,7},{6,4},{7,5},{8,10},{9,11},{10,... | collective-permute-start | bytes 399368 | tf_op jit(solution)/shard_map/ppermute | solution.py:272
  18.2 8.7 %collective-permute-done.7 = bf16[8,8320]{1,0:T(8,128)(2,1)S(1)} collective-permute-done((bf16[8,8320]{1,0:T(8,128)(2,1)S(1)}, bf16[8,8320]{1,0:T(8,128)(2,1)S(1)}, u32[]{:S(2)}, u32[]{:S(2)}) %collective-permute-start.7) | collective-permute-done | bytes 133152 | tf_op jit(solution)/shard_map/ppermute | solution.py:272
  27.5 6.6 %collective-permute-done.9 = bf16[8,8320]{1,0:T(8,128)(2,1)S(1)} collective-permute-done((bf16[8,8320]{1,0:T(8,128)(2,1)S(1)}, bf16[8,8320]{1,0:T(8,128)(2,1)S(1)}, u32[]{:S(2)}, u32[]{:S(2)}) %collective-permute-start.9) | collective-permute-done | bytes 133152 | tf_op jit(solution)/shard_map/ppermute | solution.py:272
  42.5 1.6 %collective-permute-start.12 = (s32[8,128]{1,0:T(8,128)S(1)}, s32[8,128]{1,0:T(8,128)S(1)}, u32[]{:S(2)}, u32[]{:S(2)}) collective-permute-start(s32[8,128]{1,0:T(8,128)S(1)} %broadcast_in_dim.27), channel_id=1, source_target_pairs={{0,16},{16,0},{1,17},{17,1},{2,18},{18,2},{3,19},{19,3},{4,20},{20... | collective-permute-start | bytes 12296 | tf_op jit(solution)/shard_map/ppermute | solution.py:275
  44.2 2.0 %collective-permute-done.12 = s32[8,128]{1,0:T(8,128)S(1)} collective-permute-done((s32[8,128]{1,0:T(8,128)S(1)}, s32[8,128]{1,0:T(8,128)S(1)}, u32[]{:S(2)}, u32[]{:S(2)}) %collective-permute-start.12) | collective-permute-done | bytes 4128 | tf_op jit(solution)/shard_map/ppermute | solution.py:275
  46.2 6.1 %base.2 = (f32[128,1792]{1,0:T(8,128)S(1)}, f32[128,1792]{1,0:T(8,128)S(1)}) custom-call(bf16[32,8320]{1,0:T(8,128)(2,1)S(1)} %pad_maximum_fusion.1.refs_0_, bf16[32,8320]{1,0:T(8,128)(2,1)S(1)} %constant_dynamic-update-slice_fusion.refs_1_, bf16[32,8320]{1,0:T(8,128)(2,1)S(1)} %collective-permute-done.10.refs_2_, ...), custom_call_target="tpu_custom_call" | custom-call | flops 1879048192 | bytes 14680064 | tf_op jit(solution)/shard_map/base/pallas_call | solution.py:208
  55.3 1.6 %collective-permute-start.21 = (bf16[64,3584]{1,0:T(8,128)(2,1)}, bf16[64,3584]{1,0:T(8,128)(2,1)S(1)}, u32[]{:S(2)}, u32[]{:S(2)}) collective-permute-start(bf16[64,3584]{1,0:T(8,128)(2,1)} %copy-done.6), channel_id=1, source_target_pairs={{0,1},{1,0},{2,3},{3,2},{4,5},{5,4},{6,7},{7,6},{8,9},{9,8},{10,11... | collective-permute-start | bytes 1376264 | tf_op jit(solution)/shard_map/ppermute | solution.py:272
  58.4 1.5 %collective-permute-start.23 = (bf16[32,3584]{1,0:T(8,128)(2,1)}, bf16[32,3584]{1,0:T(8,128)(2,1)S(1)}, u32[]{:S(2)}, u32[]{:S(2)}) collective-permute-start(bf16[32,3584]{1,0:T(8,128)(2,1)} %collective-permute-done.22.refs_2_), channel_id=1, source_target_pairs={{0,16},{16,0},{1,17},{17,1},{2,18},{18,2},{3,19},{19,3},{4,20},{20... | collective-permute-start | bytes 688136 | tf_op jit(solution)/shard_map/ppermute | solution.py:275
  60.6 5.0 %collective-permute-done.17.refs_2_ = bf16[32,3584]{1,0:T(8,128)(2,1)S(1)} collective-permute-done((bf16[32,3584]{1,0:T(8,128)(2,1)}, bf16[32,3584]{1,0:T(8,128)(2,1)S(1)}, u32[]{:S(2)}, u32[]{:S(2)}) %collective-permute-start.17) | collective-permute-done | bytes 229408 | tf_op jit(solution)/shard_map/ppermute | solution.py:272
  65.6 1.5 %collective-permute-start.25 = (bf16[32,3584]{1,0:T(8,128)(2,1)}, bf16[32,3584]{1,0:T(8,128)(2,1)S(1)}, u32[]{:S(2)}, u32[]{:S(2)}) collective-permute-start(bf16[32,3584]{1,0:T(8,128)(2,1)} %collective-permute-done.24.refs_4_), channel_id=1, source_target_pairs={{0,16},{16,0},{1,17},{17,1},{2,18},{18,2},{3,19},{19,3},{4,20},{20... | collective-permute-start | bytes 688136 | tf_op jit(solution)/shard_map/ppermute | solution.py:275
  67.1 1.7 %collective-permute-done.19.refs_4_ = bf16[32,3584]{1,0:T(8,128)(2,1)S(1)} collective-permute-done((bf16[32,3584]{1,0:T(8,128)(2,1)S(1)}, bf16[32,3584]{1,0:T(8,128)(2,1)S(1)}, u32[]{:S(2)}, u32[]{:S(2)}) %collective-permute-start.19) | collective-permute-done | bytes 229408 | tf_op jit(solution)/shard_map/ppermute | solution.py:272
  68.8 1.5 %collective-permute-start.18 = (bf16[32,3584]{1,0:T(8,128)(2,1)S(1)}, bf16[32,3584]{1,0:T(8,128)(2,1)S(1)}, u32[]{:S(2)}, u32[]{:S(2)}) collective-permute-start(bf16[32,3584]{1,0:T(8,128)(2,1)S(1)} %collective-permute-done.17.refs_2_), channel_id=1, source_target_pairs={{0,16},{16,0},{1,17},{17,1},{2,18},{18,2},{3,19},{19,3},{4,20},{20... | collective-permute-start | bytes 688136 | tf_op jit(solution)/shard_map/ppermute | solution.py:275
  71.9 1.5 %delta_rows.7 = (bf16[64,1792]{1,0:T(8,128)(2,1)S(1)}, bf16[64,1792]{1,0:T(8,128)(2,1)S(1)}) custom-call(bf16[64,256]{1,0:T(8,128)(2,1)S(1)} %slice.63.e_ref, bf16[64,3584]{1,0:T(8,128)(2,1)S(1)} %copy-done.8, bf16[64,3584]{1,0:T(8,128)(2,1)S(1)} %collective-permute-done.21.refs_1_, bf16[32,3584]{1,0:T(8,128)(2,1)} %collective-permute-done.22.refs_2_, ...), custom_call_target="tpu_custom_call" | custom-call | flops 117440512 | bytes 2293760 | tf_op jit(solution)/shard_map/delta_rows/pallas_call | solution.py:138
  73.4 3.9 %collective-permute-done.18.refs_3_ = bf16[32,3584]{1,0:T(8,128)(2,1)S(1)} collective-permute-done((bf16[32,3584]{1,0:T(8,128)(2,1)S(1)}, bf16[32,3584]{1,0:T(8,128)(2,1)S(1)}, u32[]{:S(2)}, u32[]{:S(2)}) %collective-permute-start.18) | collective-permute-done | bytes 229408 | tf_op jit(solution)/shard_map/ppermute | solution.py:275
  77.3 4.9 %collective-permute-done.20.refs_5_ = bf16[32,3584]{1,0:T(8,128)(2,1)S(1)} collective-permute-done((bf16[32,3584]{1,0:T(8,128)(2,1)S(1)}, bf16[32,3584]{1,0:T(8,128)(2,1)S(1)}, u32[]{:S(2)}, u32[]{:S(2)}) %collective-permute-start.20) | collective-permute-done | bytes 229408 | tf_op jit(solution)/shard_map/ppermute | solution.py:275
  82.7 1.6 %collective-permute-start.26 = (bf16[64,1792]{1,0:T(8,128)(2,1)S(1)}, bf16[64,1792]{1,0:T(8,128)(2,1)S(1)}, u32[]{:S(2)}, u32[]{:S(2)}) collective-permute-start(bf16[64,1792]{1,0:T(8,128)(2,1)S(1)} %get-tuple-element.199), channel_id=1, source_target_pairs={{0,4},{1,5},{2,6},{3,7},{4,0},{5,1},{6,2},{7,3},{8,12},{9,13},{10,... | collective-permute-start | bytes 688136 | tf_op jit(solution)/shard_map/ppermute | solution.py:272
  84.3 1.7 %collective-permute-start.27 = (bf16[64,1792]{1,0:T(8,128)(2,1)S(1)}, bf16[64,1792]{1,0:T(8,128)(2,1)S(1)}, u32[]{:S(2)}, u32[]{:S(2)}) collective-permute-start(bf16[64,1792]{1,0:T(8,128)(2,1)S(1)} %get-tuple-element.200), channel_id=1, source_target_pairs={{0,8},{1,9},{2,10},{3,11},{4,12},{5,13},{6,14},{7,15},{8,0},{9,1},... | collective-permute-start | bytes 688136 | tf_op jit(solution)/shard_map/ppermute | solution.py:272
  87.1 14.6 %base.3 = (f32[128,1792]{1,0:T(8,128)S(1)}, f32[128,1792]{1,0:T(8,128)S(1)}) custom-call(bf16[32,8320]{1,0:T(8,128)(2,1)S(1)} %pad_maximum_fusion.1.refs_0_, bf16[32,8320]{1,0:T(8,128)(2,1)S(1)} %constant_dynamic-update-slice_fusion.refs_1_, bf16[32,8320]{1,0:T(8,128)(2,1)S(1)} %collective-permute-done.10.refs_2_, ...), custom_call_target="tpu_custom_call" | custom-call | flops 5637144576 | bytes 44040192 | tf_op jit(solution)/shard_map/base/pallas_call | solution.py:208
  101.7 1.8 %collective-permute-done.27 = bf16[64,1792]{1,0:T(8,128)(2,1)S(1)} collective-permute-done((bf16[64,1792]{1,0:T(8,128)(2,1)S(1)}, bf16[64,1792]{1,0:T(8,128)(2,1)S(1)}, u32[]{:S(2)}, u32[]{:S(2)}) %collective-permute-start.27) | collective-permute-done | bytes 229408 | tf_op jit(solution)/shard_map/ppermute | solution.py:272
  (103 shorter events, 25.7 us)
Async XLA Ops:
  1.7 14.2 %collective-permute-start.6 = (bf16[8,8320]{1,0:T(8,128)(2,1)S(1)}, bf16[8,8320]{1,0:T(8,128)(2,1)S(1)}, u32[]{:S(2)}, u32[]{:S(2)}) collective-permute-start(bf16[8,8320]{1,0:T(8,128)(2,1)S(1)} %pad_maximum_fusion.2), channel_id=1, source_target_pairs={{0,8},{1,9},{2,10},{3,11},{4,12},{5,13},{6,14},{7,15},{8,0},{9,1},... | collective-permute-start | bytes 399368 | tf_op jit(solution)/shard_map/ppermute | solution.py:272
  5.8 12.0 %collective-permute-start.8 = (bf16[8,8320]{1,0:T(8,128)(2,1)S(1)}, bf16[8,8320]{1,0:T(8,128)(2,1)S(1)}, u32[]{:S(2)}, u32[]{:S(2)}) collective-permute-start(bf16[8,8320]{1,0:T(8,128)(2,1)S(1)} %pad_maximum_fusion.2), channel_id=1, source_target_pairs={{0,12},{1,13},{2,14},{3,15},{4,8},{5,9},{6,10},{7,11},{8,4},{9,5},... | collective-permute-start | bytes 399368 | tf_op jit(solution)/shard_map/ppermute | solution.py:272
  7.2 10.7 %collective-permute-start.4 = (bf16[8,8320]{1,0:T(8,128)(2,1)S(1)}, bf16[8,8320]{1,0:T(8,128)(2,1)S(1)}, u32[]{:S(2)}, u32[]{:S(2)}) collective-permute-start(bf16[8,8320]{1,0:T(8,128)(2,1)S(1)} %pad_maximum_fusion.2), channel_id=1, source_target_pairs={{0,4},{1,5},{2,6},{3,7},{4,0},{5,1},{6,2},{7,3},{8,12},{9,13},{10,... | collective-permute-start | bytes 399368 | tf_op jit(solution)/shard_map/ppermute | solution.py:272
  7.4 26.7 %collective-permute-start.3 = (bf16[8,8320]{1,0:T(8,128)(2,1)S(1)}, bf16[8,8320]{1,0:T(8,128)(2,1)S(1)}, u32[]{:S(2)}, u32[]{:S(2)}) collective-permute-start(bf16[8,8320]{1,0:T(8,128)(2,1)S(1)} %pad_maximum_fusion.2), channel_id=1, source_target_pairs={{0,2},{1,3},{2,0},{3,1},{4,6},{5,7},{6,4},{7,5},{8,10},{9,11},{10,... | collective-permute-start | bytes 399368 | tf_op jit(solution)/shard_map/ppermute | solution.py:272
  15.3 40.0 %collective-permute-start.22 = (bf16[32,3584]{1,0:T(8,128)(2,1)}, bf16[32,3584]{1,0:T(8,128)(2,1)}, u32[]{:S(2)}, u32[]{:S(2)}) collective-permute-start(bf16[32,3584]{1,0:T(8,128)(2,1)} %get-tuple-element.186), channel_id=1, source_target_pairs={{0,2},{1,3},{2,0},{3,1},{4,6},{5,7},{6,4},{7,5},{8,10},{9,11},{10,... | collective-permute-start | bytes 688136 | tf_op jit(solution)/shard_map/ppermute | solution.py:272
  16.0 10.9 %collective-permute-start.7 = (bf16[8,8320]{1,0:T(8,128)(2,1)S(1)}, bf16[8,8320]{1,0:T(8,128)(2,1)S(1)}, u32[]{:S(2)}, u32[]{:S(2)}) collective-permute-start(bf16[8,8320]{1,0:T(8,128)(2,1)S(1)} %collective-permute-done.6), channel_id=1, source_target_pairs={{0,2},{1,3},{2,0},{3,1},{4,6},{5,7},{6,4},{7,5},{8,10},{9,11},{10,... | collective-permute-start | bytes 399368 | tf_op jit(solution)/shard_map/ppermute | solution.py:272
  17.8 42.2 %collective-permute-start.24 = (bf16[32,3584]{1,0:T(8,128)(2,1)}, bf16[32,3584]{1,0:T(8,128)(2,1)}, u32[]{:S(2)}, u32[]{:S(2)}) collective-permute-start(bf16[32,3584]{1,0:T(8,128)(2,1)} %get-tuple-element.187), channel_id=1, source_target_pairs={{0,3},{1,2},{2,1},{3,0},{4,7},{5,6},{6,5},{7,4},{8,11},{9,10},{10,... | collective-permute-start | bytes 688136 | tf_op jit(solution)/shard_map/ppermute | solution.py:272
  17.9 16.1 %collective-permute-start.9 = (bf16[8,8320]{1,0:T(8,128)(2,1)S(1)}, bf16[8,8320]{1,0:T(8,128)(2,1)S(1)}, u32[]{:S(2)}, u32[]{:S(2)}) collective-permute-start(bf16[8,8320]{1,0:T(8,128)(2,1)S(1)} %collective-permute-done.8), channel_id=1, source_target_pairs={{0,2},{1,3},{2,0},{3,1},{4,6},{5,7},{6,4},{7,5},{8,10},{9,11},{10,... | collective-permute-start | bytes 399368 | tf_op jit(solution)/shard_map/ppermute | solution.py:272
  26.9 8.6 %collective-permute-start.5 = (bf16[8,8320]{1,0:T(8,128)(2,1)S(1)}, bf16[8,8320]{1,0:T(8,128)(2,1)S(1)}, u32[]{:S(2)}, u32[]{:S(2)}) collective-permute-start(bf16[8,8320]{1,0:T(8,128)(2,1)S(1)} %collective-permute-done.4), channel_id=1, source_target_pairs={{0,2},{1,3},{2,0},{3,1},{4,6},{5,7},{6,4},{7,5},{8,10},{9,11},{10,... | collective-permute-start | bytes 399368 | tf_op jit(solution)/shard_map/ppermute | solution.py:272
  40.4 16.5 %collective-permute-start.13 = (bf16[128,64]{1,0:T(8,128)(2,1)S(1)}, bf16[128,64]{1,0:T(8,128)(2,1)S(1)}, u32[]{:S(2)}, u32[]{:S(2)}) collective-permute-start(bf16[128,64]{1,0:T(8,128)(2,1)S(1)} %convolution_convert_fusion), channel_id=1, source_target_pairs={{0,1},{1,0},{2,3},{3,2},{4,5},{5,4},{6,7},{7,6},{8,9},{9,8},{10,11... | collective-permute-start | bytes 49160 | tf_op jit(solution)/shard_map/ppermute | solution.py:272
  40.6 16.9 %collective-permute-start.14 = (bf16[128,64]{1,0:T(8,128)(2,1)S(1)}, bf16[128,64]{1,0:T(8,128)(2,1)S(1)}, u32[]{:S(2)}, u32[]{:S(2)}) collective-permute-start(bf16[128,64]{1,0:T(8,128)(2,1)S(1)} %convolution_convert_fusion), channel_id=1, source_target_pairs={{0,2},{1,3},{2,0},{3,1},{4,6},{5,7},{6,4},{7,5},{8,10},{9,11},{10,... | collective-permute-start | bytes 49160 | tf_op jit(solution)/shard_map/ppermute | solution.py:272
  42.5 3.7 %collective-permute-start.12 = (s32[8,128]{1,0:T(8,128)S(1)}, s32[8,128]{1,0:T(8,128)S(1)}, u32[]{:S(2)}, u32[]{:S(2)}) collective-permute-start(s32[8,128]{1,0:T(8,128)S(1)} %broadcast_in_dim.27), channel_id=1, source_target_pairs={{0,16},{16,0},{1,17},{17,1},{2,18},{18,2},{3,19},{19,3},{4,20},{20... | collective-permute-start | bytes 12296 | tf_op jit(solution)/shard_map/ppermute | solution.py:275
  46.2 12.2 %collective-permute-start.15 = (bf16[128,64]{1,0:T(8,128)(2,1)S(1)}, bf16[128,64]{1,0:T(8,128)(2,1)S(1)}, u32[]{:S(2)}, u32[]{:S(2)}) collective-permute-start(bf16[128,64]{1,0:T(8,128)(2,1)S(1)} %convolution_convert_fusion), channel_id=1, source_target_pairs={{0,3},{1,2},{2,1},{3,0},{4,7},{5,6},{6,5},{7,4},{8,11},{9,10},{10,... | collective-permute-start | bytes 49160 | tf_op jit(solution)/shard_map/ppermute | solution.py:272
  55.3 16.6 %collective-permute-start.21 = (bf16[64,3584]{1,0:T(8,128)(2,1)}, bf16[64,3584]{1,0:T(8,128)(2,1)S(1)}, u32[]{:S(2)}, u32[]{:S(2)}) collective-permute-start(bf16[64,3584]{1,0:T(8,128)(2,1)} %copy-done.6), channel_id=1, source_target_pairs={{0,1},{1,0},{2,3},{3,2},{4,5},{5,4},{6,7},{7,6},{8,9},{9,8},{10,11... | collective-permute-start | bytes 1376264 | tf_op jit(solution)/shard_map/ppermute | solution.py:272
  57.0 8.7 %collective-permute-start.17 = (bf16[32,3584]{1,0:T(8,128)(2,1)}, bf16[32,3584]{1,0:T(8,128)(2,1)S(1)}, u32[]{:S(2)}, u32[]{:S(2)}) collective-permute-start(bf16[32,3584]{1,0:T(8,128)(2,1)} %copy-done.7), channel_id=1, source_target_pairs={{0,2},{1,3},{2,0},{3,1},{4,6},{5,7},{6,4},{7,5},{8,10},{9,11},{10,... | collective-permute-start | bytes 688136 | tf_op jit(solution)/shard_map/ppermute | solution.py:272
  57.5 11.3 %collective-permute-start.19 = (bf16[32,3584]{1,0:T(8,128)(2,1)S(1)}, bf16[32,3584]{1,0:T(8,128)(2,1)S(1)}, u32[]{:S(2)}, u32[]{:S(2)}) collective-permute-start(bf16[32,3584]{1,0:T(8,128)(2,1)S(1)} %get-tuple-element.183), channel_id=1, source_target_pairs={{0,3},{1,2},{2,1},{3,0},{4,7},{5,6},{6,5},{7,4},{8,11},{9,10},{10,... | collective-permute-start | bytes 688136 | tf_op jit(solution)/shard_map/ppermute | solution.py:272
  58.4 11.9 %collective-permute-start.23 = (bf16[32,3584]{1,0:T(8,128)(2,1)}, bf16[32,3584]{1,0:T(8,128)(2,1)S(1)}, u32[]{:S(2)}, u32[]{:S(2)}) collective-permute-start(bf16[32,3584]{1,0:T(8,128)(2,1)} %collective-permute-done.22.refs_2_), channel_id=1, source_target_pairs={{0,16},{16,0},{1,17},{17,1},{2,18},{18,2},{3,19},{19,3},{4,20},{20... | collective-permute-start | bytes 688136 | tf_op jit(solution)/shard_map/ppermute | solution.py:275
  60.0 22.2 %collective-permute-start.16 = (bf16[64,3584]{1,0:T(8,128)(2,1)}, bf16[64,3584]{1,0:T(8,128)(2,1)S(1)}, u32[]{:S(2)}, u32[]{:S(2)}) collective-permute-start(bf16[64,3584]{1,0:T(8,128)(2,1)} %copy-done.5), channel_id=1, source_target_pairs={{0,1},{1,0},{2,3},{3,2},{4,5},{5,4},{6,7},{7,6},{8,9},{9,8},{10,11... | collective-permute-start | bytes 1376264 | tf_op jit(solution)/shard_map/ppermute | solution.py:272
  65.6 6.3 %collective-permute-start.25 = (bf16[32,3584]{1,0:T(8,128)(2,1)}, bf16[32,3584]{1,0:T(8,128)(2,1)S(1)}, u32[]{:S(2)}, u32[]{:S(2)}) collective-permute-start(bf16[32,3584]{1,0:T(8,128)(2,1)} %collective-permute-done.24.refs_4_), channel_id=1, source_target_pairs={{0,16},{16,0},{1,17},{17,1},{2,18},{18,2},{3,19},{19,3},{4,20},{20... | collective-permute-start | bytes 688136 | tf_op jit(solution)/shard_map/ppermute | solution.py:275
  68.8 8.5 %collective-permute-start.18 = (bf16[32,3584]{1,0:T(8,128)(2,1)S(1)}, bf16[32,3584]{1,0:T(8,128)(2,1)S(1)}, u32[]{:S(2)}, u32[]{:S(2)}) collective-permute-start(bf16[32,3584]{1,0:T(8,128)(2,1)S(1)} %collective-permute-done.17.refs_2_), channel_id=1, source_target_pairs={{0,16},{16,0},{1,17},{17,1},{2,18},{18,2},{3,19},{19,3},{4,20},{20... | collective-permute-start | bytes 688136 | tf_op jit(solution)/shard_map/ppermute | solution.py:275
  70.3 11.9 %collective-permute-start.20 = (bf16[32,3584]{1,0:T(8,128)(2,1)S(1)}, bf16[32,3584]{1,0:T(8,128)(2,1)S(1)}, u32[]{:S(2)}, u32[]{:S(2)}) collective-permute-start(bf16[32,3584]{1,0:T(8,128)(2,1)S(1)} %collective-permute-done.19.refs_4_), channel_id=1, source_target_pairs={{0,16},{16,0},{1,17},{17,1},{2,18},{18,2},{3,19},{19,3},{4,20},{20... | collective-permute-start | bytes 688136 | tf_op jit(solution)/shard_map/ppermute | solution.py:275
  82.7 19.1 %collective-permute-start.26 = (bf16[64,1792]{1,0:T(8,128)(2,1)S(1)}, bf16[64,1792]{1,0:T(8,128)(2,1)S(1)}, u32[]{:S(2)}, u32[]{:S(2)}) collective-permute-start(bf16[64,1792]{1,0:T(8,128)(2,1)S(1)} %get-tuple-element.199), channel_id=1, source_target_pairs={{0,4},{1,5},{2,6},{3,7},{4,0},{5,1},{6,2},{7,3},{8,12},{9,13},{10,... | collective-permute-start | bytes 688136 | tf_op jit(solution)/shard_map/ppermute | solution.py:272
  84.3 19.2 %collective-permute-start.27 = (bf16[64,1792]{1,0:T(8,128)(2,1)S(1)}, bf16[64,1792]{1,0:T(8,128)(2,1)S(1)}, u32[]{:S(2)}, u32[]{:S(2)}) collective-permute-start(bf16[64,1792]{1,0:T(8,128)(2,1)S(1)} %get-tuple-element.200), channel_id=1, source_target_pairs={{0,8},{1,9},{2,10},{3,11},{4,12},{5,13},{6,14},{7,15},{8,0},{9,1},... | collective-permute-start | bytes 688136 | tf_op jit(solution)/shard_map/ppermute | solution.py:272
  85.9 17.6 %collective-permute-start.28 = (bf16[64,1792]{1,0:T(8,128)(2,1)S(1)}, bf16[64,1792]{1,0:T(8,128)(2,1)S(1)}, u32[]{:S(2)}, u32[]{:S(2)}) collective-permute-start(bf16[64,1792]{1,0:T(8,128)(2,1)S(1)} %get-tuple-element.201), channel_id=1, source_target_pairs={{0,12},{1,13},{2,14},{3,15},{4,8},{5,9},{6,10},{7,11},{8,4},{9,5},... | collective-permute-start | bytes 688136 | tf_op jit(solution)/shard_map/ppermute | solution.py:272
  (19 other events, 153.5 us)

commit v3 on v2

--- a/solution.py
+++ b/solution.py
@@ -61,34 +61,33 @@
 
 ANY = pl.BlockSpec(memory_space=pl.ANY)
 VMEM = pl.BlockSpec(memory_space=pltpu.VMEM)
-CHUNKS = ((2, 3), (1, 0))
-ROOM = 64
-
-
-def repack_kernel(width, u_ref, *refs):
-    outs, (held, in_sems, out_sems) = refs[:-3], refs[-3:]
-    half = u_ref.shape[0] // 2
+ROOMS = (64, 16, 48)
+FACTORS = (2, 3)
+ROWS = (0, 1)
+BLOCKS = PLANES + len(ROWS)
+
+
+def repack_kernel(width, u_ref, own_ref, core_ref, cross_ref, both_ref, held, in_sems, out_sems):
+    rank = u_ref.shape[0]
+    half = rank // 2
     me, y = lax.axis_index("dp"), lax.axis_index("groups")
     z, x, c = me // 4, (me // 2) % 2, me % 2
     ins, sends = [], []
-    for k, chunk in enumerate(CHUNKS):
-        own, core, cross, both = outs[4 * k : 4 * k + 4]
-        for ref, xx, cc, split in (
-            (cross, 1 - x, c, True),
-            (both, 1 - x, 1 - c, True),
-            (core, x, 1 - c, False),
-            (own, x, c, False),
-        ):
-            for i, j in enumerate(chunk):
-                zz = lax.bitwise_xor(z, j)
-                n = len(ins)
-                at = pl.multiple_of(((zz * 2 + xx) * 2 + cc) * width, LANES)
-                rows = pl.ds(pl.multiple_of(y * half, half), half) if split else pl.ds(0, 2 * half)
-                here = held.at[pl.ds(0, half if split else 2 * half), pl.ds(n * width, width)]
-                ins.append(pltpu.make_async_copy(u_ref.at[rows, pl.ds(at, width)], here, in_sems.at[n]))
-                sends.append(
-                    pltpu.make_async_copy(here, ref.at[:, pl.ds(i * width, width)], out_sems.at[n])
-                )
+
+    def move(j, xx, cc, split, target):
+        n = len(ins)
+        at = pl.multiple_of(((lax.bitwise_xor(z, j) * 2 + xx) * 2 + cc) * width, LANES)
+        rows = pl.ds(pl.multiple_of(y * half, half), half) if split else pl.ds(0, rank)
+        here = held.at[pl.ds(0, half if split else rank), pl.ds(n * width, width)]
+        ins.append(pltpu.make_async_copy(u_ref.at[rows, pl.ds(at, width)], here, in_sems.at[n]))
+        sends.append(pltpu.make_async_copy(here, target, out_sems.at[n]))
+
+    for i, j in enumerate(FACTORS):
+        move(j, 1 - x, c, True, cross_ref.at[:, pl.ds(i * width, width)])
+        move(j, 1 - x, 1 - c, True, both_ref.at[:, pl.ds(i * width, width)])
+    for cc, ref in ((1 - c, core_ref), (c, own_ref)):
+        for i, (j, xx) in enumerate([(j, x) for j in range(PLANES)] + [(j, 1 - x) for j in ROWS]):
+            move(j, xx, cc, False, ref.at[:, pl.ds(i * width, width)])
     for copy in ins:
         copy.start()
     for copy, send in zip(ins, sends):
@@ -100,15 +99,9 @@
 
 def repack(u, width):
     rank = u.shape[0]
-    shapes = []
-    for chunk in CHUNKS:
-        n = len(chunk) * width
-        shapes += [
-            jax.ShapeDtypeStruct((rank, n), BF16),
-            jax.ShapeDtypeStruct((rank, n), BF16),
-            jax.ShapeDtypeStruct((rank // 2, n), BF16),
-            jax.ShapeDtypeStruct((rank // 2, n), BF16),
-        ]
+    wide = jax.ShapeDtypeStruct((rank, BLOCKS * width), BF16)
+    split = jax.ShapeDtypeStruct((rank // 2, len(FACTORS) * width), BF16)
+    shapes = [wide, wide, split, split]
     return pl.pallas_call(
         functools.partial(repack_kernel, width),
         out_shape=shapes,
@@ -125,18 +118,20 @@
     )(u)
 
 
-def delta_kernel(width, e_ref, *refs):
-    parts, outs = refs[:6], refs[6:]
-    for i, out in enumerate(outs):
-        stacked = jnp.concatenate([ref[:, i * width : (i + 1) * width] for ref in parts], axis=0)
-        out[...] = jnp.dot(e_ref[...], stacked, preferred_element_type=F32).astype(BF16)
-
-
-def delta_rows(e, parts, width):
+def delta_kernel(plan, width, e_ref, *refs):
+    parts, outs = refs[: len(refs) - len(plan)], refs[len(refs) - len(plan) :]
+    for pieces, out in zip(plan, outs):
+        stacked = jnp.concatenate(
+            [parts[n][:rows, i * width : (i + 1) * width] for n, i, rows in pieces], axis=0
+        )
+        out[...] = jnp.dot(e_ref[:, : stacked.shape[0]], stacked, preferred_element_type=F32).astype(BF16)
+
+
+def delta_rows(e, parts, plan, width):
     rows = e.shape[0]
-    n = parts[0].shape[1] // width
+    n = len(plan)
     return pl.pallas_call(
-        functools.partial(delta_kernel, width),
+        functools.partial(delta_kernel, plan, width),
         out_shape=[jax.ShapeDtypeStruct((rows, width), BF16)] * n,
         in_specs=[VMEM] * (1 + len(parts)),
         out_specs=[VMEM] * n,
@@ -276,80 +271,81 @@
 
     ids = jnp.broadcast_to(token_adapter_index.astype(BF16), (own_rows, LANES))
     packed = jnp.concatenate([tokens, ids], axis=1)
-    by_plane = [packed] + [swap(packed, 4 * j) for j in range(1, PLANES)]
-    near = [
-        jnp.concatenate([p for q in by_plane[i : i + 2] for p in (q, swap(q, 2))], axis=0) for i in (0, 2)
-    ]
-    x_parts = (*near, *[swap(v, 1) for v in near])
-
-    pieces = repack(adapter_up_factor[0], width)
-    stacks = []
-    for k in range(len(CHUNKS)):
-        own, core, cross, both = pieces[4 * k : 4 * k + 4]
-        cross, both = swap(cross, 2), swap(both, 3)
-        stacks.append((own, swap(core, 1), cross, other(cross), both, other(both)))
+    second, third = swap(packed, 8), swap(packed, 12)
+    pair = jnp.concatenate([packed, swap(packed, 2)], axis=0)
+    close = jnp.concatenate([pair, swap(pair, 4)], axis=0)
+    remote = jnp.concatenate([second, third], axis=0)
+    remote = jnp.concatenate([remote, swap(remote, 2)], axis=0)
+    x_parts = (close, remote, swap(close, 1), swap(remote, 1))
+    distances = [0, 2, 4, 6, 8, 12, 10, 14]
+    distances = distances + [k + 1 for k in distances]
+
+    own, core, cross, both = repack(adapter_up_factor[0], width)
+    core = swap(core, 1)
+    cross, both = swap(cross, 2), swap(both, 3)
+    cross_parts = (cross, other(cross), both, other(both))
+    half = rank // 2
 
     place = jnp.arange(total, dtype=jnp.int32)
-    block = place // own_rows
-    distance = (block % 8) * 2 + block // 8
-    order_of = (distance ^ me) * own_rows + place % own_rows
+    order_of = (jnp.repeat(jnp.array(distances, jnp.int32), own_rows) ^ me) * own_rows + place % own_rows
     all_ids = jnp.concatenate([v[:, depth] for v in x_parts]).astype(jnp.int32)
     adapters = jnp.arange(count, dtype=jnp.int32)
     slots = jnp.sum(jnp.where(all_ids[:, None] == adapters[None, :], adapter_slot_index[None, :], 0), 1)
     planes = slots // 4
     before = (planes[None, :] == planes[:, None]) & (order_of[None, :] < order_of[:, None])
     ranks = jnp.sum(before.astype(jnp.int32), 1)
-    most = jnp.max(ranks)
-    all_most = jnp.maximum(most, jnp.max(other(jnp.broadcast_to(most, (8, LANES)))))
 
     low = jnp.concatenate(
         [jnp.dot(v[:, :depth], adapter_down_factor[0], preferred_element_type=F32) for v in x_parts], axis=0
     ).astype(BF16)
-    mine = (slots == me)[None, :] & (ranks[None, :] == place[:, None])
-    low = jnp.dot(mine.astype(BF16), low, preferred_element_type=F32).astype(BF16)
-    low, x_parts = lax.optimization_barrier((low, x_parts))
+    mine = ((slots == me)[None, :] & (ranks[None, :] == place[:, None])).astype(BF16)
+    low = jnp.dot(mine, low, preferred_element_type=F32).astype(BF16)
+    low, x_parts, slots, ranks = lax.optimization_barrier((low, x_parts, slots, ranks))
 
     def turned(v):
-        return jnp.where(y == 0, v, jnp.concatenate([v[:, rank // 2 :], v[:, : rank // 2]], axis=1))
-
-    lows = [low, swap(low, 1), swap(low, 2), swap(low, 3)]
-    steps = depth // BLOCK
-    early = steps // 4
-    sums = base(x_parts, gate_matrix, up_matrix, 0, early)
-    lows, sums = lax.optimization_barrier((lows, sums))
-    e = jnp.concatenate([lows[0], lows[1], turned(lows[2]), turned(lows[3])], axis=1)
-
-    def rows_of(e):
-        by_plane = {}
-        for chunk, parts in zip(CHUNKS, stacks):
-            by_plane.update(zip(chunk, delta_rows(e, parts, width)))
-        return [by_plane[j] for j in range(PLANES)]
-
-    def sent(rows):
-        return [rows[0]] + [swap(rows[j], 4 * j) for j in (1, 2, 3)]
-
-    rows, sums = lax.optimization_barrier((rows_of(e[:ROOM]), sums))
-    rows = sent(rows)
-    gate, up = base(x_parts, gate_matrix, up_matrix, early, steps - early, sums)
+        return jnp.where(y == 0, v, jnp.concatenate([v[:, half:], v[:, :half]], axis=1))
+
+    chip = jnp.concatenate([low, swap(low, 1)], axis=1)
+    plane = jnp.concatenate([chip, turned(swap(low, 2)), turned(swap(low, 3))], axis=1)
+    chip_plan = tuple(((0, i, rank), (1, i, rank)) for i in (0, 1, PLANES, PLANES + 1))
+    plane_plan = tuple(
+        ((0, j, rank), (1, j, rank)) + tuple((n, i, half) for n in (2, 3, 4, 5)) for i, j in enumerate(FACTORS)
+    )
+
+    def sent(start, room):
+        at = slice(start, start + room)
+        here, first, here_cross, first_cross = delta_rows(chip[at], (own, core), chip_plan, width)
+        second, third = delta_rows(plane[at], (own, core, *cross_parts), plane_plan, width)
+        return here, first, second, third, here_cross, first_cross
+
+    def arrived(rows):
+        return [rows[0]] + [swap(v, k) for v, k in zip(rows[1:], (4, 8, 12, 2, 6))]
+
+    rows, x_parts = lax.optimization_barrier((sent(0, ROOMS[0]), x_parts))
+    rows = arrived(rows)
+    gate, up = base(x_parts, gate_matrix, up_matrix, 0, depth // BLOCK)
 
     order = (order_of[None, :] == place[:, None]).astype(BF16)
-    plane = planes ^ z
-
-    def picked(room, start):
-        at = jnp.where((ranks >= start) & (ranks < start + room), plane * room + ranks - start, -1)
-        return (at[:, None] == jnp.arange(PLANES * room, dtype=jnp.int32)[None, :]).astype(BF16)
-
-    first = picked(ROOM, 0)
+    most = jnp.max(ranks) + 1
+    most = jnp.maximum(most, jnp.max(other(jnp.broadcast_to(most, (8, LANES)))))
+    branch = (most > ROOMS[0]).astype(jnp.int32) + (most > ROOMS[0] + ROOMS[1]).astype(jnp.int32)
+
+    def picked(start, room):
+        at = jnp.where((ranks >= start) & (ranks < start + room), ((slots // 4) ^ z) * room + ranks - start, -1)
+        pick = (at[:, None] == jnp.arange(PLANES * room, dtype=jnp.int32)[None, :]).astype(BF16)
+        return jnp.concatenate([pick, pick[:, : len(ROWS) * room]], axis=1)
+
+    first = picked(0, ROOMS[0])
 
     def short():
         return finish(gate, up, first, order, rows)
 
-    def long():
-        rest = sent(rows_of(e[ROOM:]))
-        pick = jnp.concatenate([first, picked(total - ROOM, ROOM)], axis=1)
+    def more(room):
+        rest = arrived(sent(ROOMS[0], room))
+        pick = jnp.concatenate([first, picked(ROOMS[0], room)], axis=1)
         return finish(gate, up, pick, order, rows + rest)
 
-    return lax.cond(all_most < ROOM, short, long)
+    return lax.switch(branch, (short, lambda: more(ROOMS[1]), lambda: more(ROOMS[1] + ROOMS[2])))
 
 
 def solution(mesh):

time: 108 us -> 77.1 us (0.71)
  waiting for transfers between devices: 36.1 us -> 11.8 us
  local copies, waits for them, and re-layouts: 9.3 us -> 4.96 us
  other arithmetic: 6 us -> 4.7 us
  starting transfers between devices: 26 us -> 24.9 us
    ppermute x21 -> x18, waiting for transfers between devices: 25.3 us -> 9.73 us  [swap(): return lax.ppermute(value, 'dp', [(d, d ^ k) for d in range(count)])]
    ppermute x5 -> x3, waiting for transfers between devices: 10.8 us -> 2.08 us  [other(): return lax.ppermute(value, 'groups', [(0, 1), (1, 0)])]
    unnamed x37 -> x20, local copies, waits for them, and re-layouts: 7.93 us -> 4.09 us
    pallas_call x2, Pallas kernels: 1.92 us -> 4.23 us  [delta_rows(): pl.pallas_call(functools.partial(delta_kernel, plan, width), out_shape=[j...]
    pallas_call x2 -> x1, Pallas kernels: 20.7 us -> 18.7 us  [base(): pl.pallas_call(functools.partial(base_kernel, first, steps, rows, bool(su...]
    ppermute x5 -> x3, starting transfers between devices: 6.65 us -> 4.62 us  [other(): return lax.ppermute(value, 'groups', [(0, 1), (1, 0)])]
    concatenate x2 -> x7, other arithmetic: 1.92 us -> 0.37 us  [the longest x2 0.17 us: plane_shards(): chip = jnp.concatenate([low, swap(low, 1)], axis=1)]
    ppermute x21 -> x18, starting transfers between devices: 19.3 us -> 20.3 us  [swap(): return lax.ppermute(value, 'dp', [(d, d ^ k) for d in range(count)])]
  transfers between devices with their start and end apart: 26 -> 21, of which waited for: 11 -> 9; matrix products, arithmetic and copies ran while one was open for 7% -> 7% of each run, Pallas kernels for 23% -> 31%
where the time goes in v3:
time: 77.1 us; the launch traced here: 76.8 us
  Pallas kernels  26.9 us (35%)
  starting transfers between devices  24.9 us (32%)
  waiting for transfers between devices  11.8 us (15%)
  local copies, waits for them, and re-layouts  4.96 us (6%)
  other arithmetic  4.7 us (6%)
  matrix products  1.76 us (2%)
  between operations  1.71 us (2%)
    ppermute x18, starting transfers between devices, swap(): return lax.ppermute(value, 'dp', [(d, d ^ k) for d in range(count)])  20.3 us
    pallas_call x1, Pallas kernels, base(): pl.pallas_call(functools.partial(base_kernel, first, steps, rows, bool(su...  18.7 us
    ppermute x18, waiting for transfers between devices, swap(): return lax.ppermute(value, 'dp', [(d, d ^ k) for d in range(count)])  9.73 us
    ppermute x3, starting transfers between devices, other(): return lax.ppermute(value, 'groups', [(0, 1), (1, 0)])  4.62 us
    pallas_call x2, Pallas kernels, delta_rows(): pl.pallas_call(functools.partial(delta_kernel, plan, width), out_shape=[j...  4.23 us
    unnamed x20, local copies, waits for them, and re-layouts  4.09 us
    pallas_call x1, Pallas kernels, repack(): pl.pallas_call(functools.partial(repack_kernel, width), out_shape=shapes,...  2.65 us
    ppermute x3, waiting for transfers between devices, other(): return lax.ppermute(value, 'groups', [(0, 1), (1, 0)])  2.08 us
  transfers between devices with their start and end apart: 21, of which 9 were waited for; matrix products, arithmetic and copies ran while one was open for 7% of the time, Pallas kernels for 31%

profile of v3, /device:TPU:0, one launch (start us, length us, event | category | flops | bytes accessed | tf_op | source)
XLA Modules:
  0.0 76.8 jit_solution(7932967228166818158)
XLA Ops:
  1.7 4.1 %collective-permute-start.12 = (bf16[8,8320]{1,0:T(8,128)(2,1)S(1)}, bf16[8,8320]{1,0:T(8,128)(2,1)S(1)}, u32[]{:S(2)}, u32[]{:S(2)}) collective-permute-start(bf16[8,8320]{1,0:T(8,128)(2,1)S(1)} %pad_maximum_fusion.5), channel_id=1, source_target_pairs={{0,8},{1,9},{2,10},{3,11},{4,12},{5,13},{6,14},{7,15},{8,0},{9,1},... | collective-permute-start | bytes 399368 | tf_op jit(solution)/shard_map/ppermute | solution.py:267
  5.8 1.3 %collective-permute-start.13 = (bf16[8,8320]{1,0:T(8,128)(2,1)S(1)}, bf16[8,8320]{1,0:T(8,128)(2,1)S(1)}, u32[]{:S(2)}, u32[]{:S(2)}) collective-permute-start(bf16[8,8320]{1,0:T(8,128)(2,1)S(1)} %pad_maximum_fusion.5), channel_id=1, source_target_pairs={{0,12},{1,13},{2,14},{3,15},{4,8},{5,9},{6,10},{7,11},{8,4},{9,5},... | collective-permute-start | bytes 399368 | tf_op jit(solution)/shard_map/ppermute | solution.py:267
  7.2 1.5 %collective-permute-start.10 = (bf16[8,8320]{1,0:T(8,128)(2,1)S(1)}, bf16[8,8320]{1,0:T(8,128)(2,1)S(1)}, u32[]{:S(2)}, u32[]{:S(2)}) collective-permute-start(bf16[8,8320]{1,0:T(8,128)(2,1)S(1)} %pad_maximum_fusion.5), channel_id=1, source_target_pairs={{0,2},{1,3},{2,0},{3,1},{4,6},{5,7},{6,4},{7,5},{8,10},{9,11},{10,... | collective-permute-start | bytes 399368 | tf_op jit(solution)/shard_map/ppermute | solution.py:267
  8.7 2.0 %copy-done.2 = bf16[1,64,28672]{2,1,0:T(8,128)(2,1)S(1)} copy-done((bf16[1,64,28672]{2,1,0:T(8,128)(2,1)S(1)}, bf16[1,64,28672]{2,1,0:T(8,128)(2,1)}, u32[]{:S(2)}) %copy-start.2) | copy-done | bytes 3670040
  10.7 2.7 %repack.1 = (bf16[64,10752]{1,0:T(8,128)(2,1)}, bf16[64,10752]{1,0:T(8,128)(2,1)}, bf16[32,3584]{1,0:T(8,128)(2,1)S(1)}, bf16[32,3584]{1,0:T(8,128)(2,1)S(1)}) custom-call(bf16[64,28672]{1,0:T(8,128)(2,1)S(1)} %bitcast.13), custom_call_target="tpu_custom_call" | custom-call | bytes 5505024 | tf_op jit(solution)/shard_map/repack/pallas_call | solution.py:105
  14.8 1.1 %collective-permute-done.12 = bf16[8,8320]{1,0:T(8,128)(2,1)S(1)} collective-permute-done((bf16[8,8320]{1,0:T(8,128)(2,1)S(1)}, bf16[8,8320]{1,0:T(8,128)(2,1)S(1)}, u32[]{:S(2)}, u32[]{:S(2)}) %collective-permute-start.12) | collective-permute-done | bytes 133152 | tf_op jit(solution)/shard_map/ppermute | solution.py:267
  16.5 1.4 %collective-permute-start.14 = (bf16[16,8320]{1,0:T(8,128)(2,1)S(1)}, bf16[16,8320]{1,0:T(8,128)(2,1)S(1)}, u32[]{:S(2)}, u32[]{:S(2)}) collective-permute-start(bf16[16,8320]{1,0:T(8,128)(2,1)S(1)} %pad_maximum_fusion.4), channel_id=1, source_target_pairs={{0,2},{1,3},{2,0},{3,1},{4,6},{5,7},{6,4},{7,5},{8,10},{9,11},{10,... | collective-permute-start | bytes 798728 | tf_op jit(solution)/shard_map/ppermute | solution.py:267
  17.9 2.5 %collective-permute-start.11 = (bf16[16,8320]{1,0:T(8,128)(2,1)S(1)}, bf16[16,8320]{1,0:T(8,128)(2,1)S(1)}, u32[]{:S(2)}, u32[]{:S(2)}) collective-permute-start(bf16[16,8320]{1,0:T(8,128)(2,1)S(1)} %pad_maximum_fusion.3), channel_id=1, source_target_pairs={{0,4},{1,5},{2,6},{3,7},{4,0},{5,1},{6,2},{7,3},{8,12},{9,13},{10,... | collective-permute-start | bytes 798728 | tf_op jit(solution)/shard_map/ppermute | solution.py:267
  20.4 1.6 %collective-permute-done.22.refs_2_ = bf16[32,3584]{1,0:T(8,128)(2,1)S(1)} collective-permute-done((bf16[32,3584]{1,0:T(8,128)(2,1)S(1)}, bf16[32,3584]{1,0:T(8,128)(2,1)S(1)}, u32[]{:S(2)}, u32[]{:S(2)}) %collective-permute-start.22) | collective-permute-done | bytes 229408 | tf_op jit(solution)/shard_map/ppermute | solution.py:267
  22.0 1.5 %collective-permute-start.23 = (bf16[32,3584]{1,0:T(8,128)(2,1)S(1)}, bf16[32,3584]{1,0:T(8,128)(2,1)}, u32[]{:S(2)}, u32[]{:S(2)}) collective-permute-start(bf16[32,3584]{1,0:T(8,128)(2,1)S(1)} %collective-permute-done.22.refs_2_), channel_id=1, source_target_pairs={{0,16},{16,0},{1,17},{17,1},{2,18},{18,2},{3,19},{19,3},{4,20},{20... | collective-permute-start | bytes 688136 | tf_op jit(solution)/shard_map/ppermute | solution.py:270
  23.5 1.4 %collective-permute-done.24.refs_4_ = bf16[32,3584]{1,0:T(8,128)(2,1)} collective-permute-done((bf16[32,3584]{1,0:T(8,128)(2,1)S(1)}, bf16[32,3584]{1,0:T(8,128)(2,1)}, u32[]{:S(2)}, u32[]{:S(2)}) %collective-permute-start.24) | collective-permute-done | bytes 229408 | tf_op jit(solution)/shard_map/ppermute | solution.py:267
  25.0 1.5 %collective-permute-start.25 = (bf16[32,3584]{1,0:T(8,128)(2,1)}, bf16[32,3584]{1,0:T(8,128)(2,1)}, u32[]{:S(2)}, u32[]{:S(2)}) collective-permute-start(bf16[32,3584]{1,0:T(8,128)(2,1)} %collective-permute-done.24.refs_4_), channel_id=1, source_target_pairs={{0,16},{16,0},{1,17},{17,1},{2,18},{18,2},{3,19},{19,3},{4,20},{20... | collective-permute-start | bytes 688136 | tf_op jit(solution)/shard_map/ppermute | solution.py:270
  26.5 4.1 %collective-permute-done.14 = bf16[16,8320]{1,0:T(8,128)(2,1)S(1)} collective-permute-done((bf16[16,8320]{1,0:T(8,128)(2,1)S(1)}, bf16[16,8320]{1,0:T(8,128)(2,1)S(1)}, u32[]{:S(2)}, u32[]{:S(2)}) %collective-permute-start.14) | collective-permute-done | bytes 266272 | tf_op jit(solution)/shard_map/ppermute | solution.py:267
  36.9 1.6 %collective-permute-start.17 = (s32[8,128]{1,0:T(8,128)S(1)}, s32[8,128]{1,0:T(8,128)S(1)}, u32[]{:S(2)}, u32[]{:S(2)}) collective-permute-start(s32[8,128]{1,0:T(8,128)S(1)} %broadcast_in_dim.29), channel_id=1, source_target_pairs={{0,16},{16,0},{1,17},{17,1},{2,18},{18,2},{3,19},{19,3},{4,20},{20... | collective-permute-start | bytes 12296 | tf_op jit(solution)/shard_map/ppermute | solution.py:270
  38.5 2.1 %collective-permute-done.17 = s32[8,128]{1,0:T(8,128)S(1)} collective-permute-done((s32[8,128]{1,0:T(8,128)S(1)}, s32[8,128]{1,0:T(8,128)S(1)}, u32[]{:S(2)}, u32[]{:S(2)}) %collective-permute-start.17) | collective-permute-done | bytes 4128 | tf_op jit(solution)/shard_map/ppermute | solution.py:270
  42.0 1.7 %collective-permute-start.18 = (bf16[128,64]{1,0:T(8,128)(2,1)S(1)}, bf16[128,64]{1,0:T(8,128)(2,1)S(1)}, u32[]{:S(2)}, u32[]{:S(2)}) collective-permute-start(bf16[128,64]{1,0:T(8,128)(2,1)S(1)} %convolution_convert_fusion), channel_id=1, source_target_pairs={{0,1},{1,0},{2,3},{3,2},{4,5},{5,4},{6,7},{7,6},{8,9},{9,8},{10,11... | collective-permute-start | bytes 49160 | tf_op jit(solution)/shard_map/ppermute | solution.py:267
  44.9 2.3 %delta_rows.10 = (bf16[64,1792]{1,0:T(8,128)(2,1)S(1)}, bf16[64,1792]{1,0:T(8,128)(2,1)S(1)}, bf16[64,1792]{1,0:T(8,128)(2,1)S(1)}, bf16[64,1792]{1,0:T(8,128)(2,1)S(1)}) custom-call(bf16[64,128]{1,0:T(8,128)(2,1)S(1)} %fusion.23.e_ref, bf16[64,10752]{1,0:T(8,128)(2,1)} %get-tuple-element.208.refs_0_, bf16[64,10752]{1,0:T(8,128)(2,1)} %collective-permute-done.19.refs_1_), custom_call_target="tpu_custom_call" | custom-call | flops 117440512 | bytes 2752512 | tf_op jit(solution)/shard_map/delta_rows/pallas_call | solution.py:133
  47.1 2.0 %delta_rows.11 = (bf16[64,1792]{1,0:T(8,128)(2,1)S(1)}, bf16[64,1792]{1,0:T(8,128)(2,1)S(1)}) custom-call(bf16[64,256]{1,0:T(8,128)(2,1)S(1)} %slice.94.e_ref, bf16[64,10752]{1,0:T(8,128)(2,1)S(1)} %copy-done.3, bf16[64,10752]{1,0:T(8,128)(2,1)} %collective-permute-done.19.refs_1_, bf16[32,3584]{1,0:T(8,128)(2,1)S(1)} %collective-permute-done.22.refs_2_, ...), custom_call_target="tpu_custom_call" | custom-call | flops 117440512 | bytes 2293760 | tf_op jit(solution)/shard_map/delta_rows/pallas_call | solution.py:133
  49.7 2.5 %collective-permute-start.27 = (bf16[64,1792]{1,0:T(8,128)(2,1)S(1)}, bf16[64,1792]{1,0:T(8,128)(2,1)S(1)}, u32[]{:S(2)}, u32[]{:S(2)}) collective-permute-start(bf16[64,1792]{1,0:T(8,128)(2,1)S(1)} %get-tuple-element.231), channel_id=1, source_target_pairs={{0,8},{1,9},{2,10},{3,11},{4,12},{5,13},{6,14},{7,15},{8,0},{9,1},... | collective-permute-start | bytes 688136 | tf_op jit(solution)/shard_map/ppermute | solution.py:267
  52.2 1.4 %collective-permute-start.28 = (bf16[64,1792]{1,0:T(8,128)(2,1)S(1)}, bf16[64,1792]{1,0:T(8,128)(2,1)S(1)}, u32[]{:S(2)}, u32[]{:S(2)}) collective-permute-start(bf16[64,1792]{1,0:T(8,128)(2,1)S(1)} %get-tuple-element.232), channel_id=1, source_target_pairs={{0,12},{1,13},{2,14},{3,15},{4,8},{5,9},{6,10},{7,11},{8,4},{9,5},... | collective-permute-start | bytes 688136 | tf_op jit(solution)/shard_map/ppermute | solution.py:267
  54.7 18.7 %base.1 = (f32[128,1792]{1,0:T(8,128)S(1)}, f32[128,1792]{1,0:T(8,128)S(1)}) custom-call(bf16[32,8320]{1,0:T(8,128)(2,1)S(1)} %pad_maximum_fusion.2.refs_0_, bf16[32,8320]{1,0:T(8,128)(2,1)S(1)} %constant_dynamic-update-slice_fusion.refs_1_, bf16[32,8320]{1,0:T(8,128)(2,1)S(1)} %collective-permute-done.15.refs_2_, ...), custom_call_target="tpu_custom_call" | custom-call | flops 7516192768 | bytes 58720256 | tf_op jit(solution)/shard_map/base/pallas_call | solution.py:203
  73.4 1.4 %conditional.1 = (bf16[128,1792]{1,0:T(8,128)(2,1)S(1)}) conditional(s32[]{:T(128)} %clamp.3, (f32[128,1792]{1,0:T(8,128)S(1)}, f32[128,1792]{1,0:T(8,128)S(1)}, bf16[128,384]{1,0:T(8,128)(2,1)S(1)}, bf16[128,128]{1,0:T(8,128)(2,1)S(1)}, bf16[64,1792]{1,0:T(8,128)(2,1)S(1)}, /*index=5*/bf16[64,1792]{1,0:T(8,128)(2,1)S(1)}, ...), branch_computations={%region_4.5_spmd, %region_5.6_spmd, %region_6.7_spmd} | conditional | flops 235539328 | bytes 13928660 | solution.py:348
  73.4 1.4 %finish.3 = bf16[128,1792]{1,0:T(8,128)(2,1)S(1)} custom-call(f32[128,1792]{1,0:T(8,128)S(1)} %get-tuple-element.112.gate_ref, f32[128,1792]{1,0:T(8,128)S(1)} %get-tuple-element.114.up_ref, bf16[128,384]{1,0:T(8,128)(2,1)S(1)} %get-tuple-element.115.pick_ref, bf16[128,128]{1,0:T(8,128)(2,1)S(1)} %get-tuple-element.116.order_ref, ...), custom_call_target="tpu_custom_call" | custom-call | bytes 3670016 | tf_op jit(solution)/shard_map/cond/branch_0_fun/finish/pallas_call | solution.py:237
  75.6 1.2 %copy-done.1 = bf16[1,8192,64]{1,2,0:T(8,128)(2,1)S(1)} copy-done((bf16[1,8192,64]{1,2,0:T(8,128)(2,1)S(1)}, bf16[1,8192,64]{1,2,0:T(8,128)(2,1)}, u32[]{:S(2)}) %copy-start.1) | copy-done | bytes 1048600
  (84 shorter events, 13.6 us)
Async XLA Ops:
  0.0 31.3 %copy-start = (bf16[1,8192,64]{1,2,0:T(8,128)(2,1)S(1)}, bf16[1,8192,64]{1,2,0:T(8,128)(2,1)}, u32[]{:S(2)}) copy-start(bf16[1,8192,64]{1,2,0:T(8,128)(2,1)} %param.16) | copy-start | bytes 3145732
  1.7 14.2 %collective-permute-start.12 = (bf16[8,8320]{1,0:T(8,128)(2,1)S(1)}, bf16[8,8320]{1,0:T(8,128)(2,1)S(1)}, u32[]{:S(2)}, u32[]{:S(2)}) collective-permute-start(bf16[8,8320]{1,0:T(8,128)(2,1)S(1)} %pad_maximum_fusion.5), channel_id=1, source_target_pairs={{0,8},{1,9},{2,10},{3,11},{4,12},{5,13},{6,14},{7,15},{8,0},{9,1},... | collective-permute-start | bytes 399368 | tf_op jit(solution)/shard_map/ppermute | solution.py:267
  5.8 10.6 %collective-permute-start.13 = (bf16[8,8320]{1,0:T(8,128)(2,1)S(1)}, bf16[8,8320]{1,0:T(8,128)(2,1)S(1)}, u32[]{:S(2)}, u32[]{:S(2)}) collective-permute-start(bf16[8,8320]{1,0:T(8,128)(2,1)S(1)} %pad_maximum_fusion.5), channel_id=1, source_target_pairs={{0,12},{1,13},{2,14},{3,15},{4,8},{5,9},{6,10},{7,11},{8,4},{9,5},... | collective-permute-start | bytes 399368 | tf_op jit(solution)/shard_map/ppermute | solution.py:267
  7.2 10.7 %collective-permute-start.10 = (bf16[8,8320]{1,0:T(8,128)(2,1)S(1)}, bf16[8,8320]{1,0:T(8,128)(2,1)S(1)}, u32[]{:S(2)}, u32[]{:S(2)}) collective-permute-start(bf16[8,8320]{1,0:T(8,128)(2,1)S(1)} %pad_maximum_fusion.5), channel_id=1, source_target_pairs={{0,2},{1,3},{2,0},{3,1},{4,6},{5,7},{6,4},{7,5},{8,10},{9,11},{10,... | collective-permute-start | bytes 399368 | tf_op jit(solution)/shard_map/ppermute | solution.py:267
  10.7 7.1 %copy-start.4 = (bf16[8,8192]{1,0:T(8,128)(2,1)S(1)}, bf16[8,8192]{1,0:T(8,128)(2,1)}, u32[]{:S(2)}) copy-start(bf16[8,8192]{1,0:T(8,128)(2,1)} %param.11) | copy-start | bytes 393220
  13.4 8.6 %collective-permute-start.22 = (bf16[32,3584]{1,0:T(8,128)(2,1)S(1)}, bf16[32,3584]{1,0:T(8,128)(2,1)S(1)}, u32[]{:S(2)}, u32[]{:S(2)}) collective-permute-start(bf16[32,3584]{1,0:T(8,128)(2,1)S(1)} %get-tuple-element.212), channel_id=1, source_target_pairs={{0,2},{1,3},{2,0},{3,1},{4,6},{5,7},{6,4},{7,5},{8,10},{9,11},{10,... | collective-permute-start | bytes 688136 | tf_op jit(solution)/shard_map/ppermute | solution.py:267
  14.0 11.0 %collective-permute-start.24 = (bf16[32,3584]{1,0:T(8,128)(2,1)S(1)}, bf16[32,3584]{1,0:T(8,128)(2,1)}, u32[]{:S(2)}, u32[]{:S(2)}) collective-permute-start(bf16[32,3584]{1,0:T(8,128)(2,1)S(1)} %get-tuple-element.213), channel_id=1, source_target_pairs={{0,3},{1,2},{2,1},{3,0},{4,7},{5,6},{6,5},{7,4},{8,11},{9,10},{10,... | collective-permute-start | bytes 688136 | tf_op jit(solution)/shard_map/ppermute | solution.py:267
  15.9 28.9 %collective-permute-start.19 = (bf16[64,10752]{1,0:T(8,128)(2,1)}, bf16[64,10752]{1,0:T(8,128)(2,1)}, u32[]{:S(2)}, u32[]{:S(2)}) collective-permute-start(bf16[64,10752]{1,0:T(8,128)(2,1)} %get-tuple-element.209), channel_id=1, source_target_pairs={{0,1},{1,0},{2,3},{3,2},{4,5},{5,4},{6,7},{7,6},{8,9},{9,8},{10,11... | collective-permute-start | bytes 4128776 | tf_op jit(solution)/shard_map/ppermute | solution.py:267
  16.5 14.1 %collective-permute-start.14 = (bf16[16,8320]{1,0:T(8,128)(2,1)S(1)}, bf16[16,8320]{1,0:T(8,128)(2,1)S(1)}, u32[]{:S(2)}, u32[]{:S(2)}) collective-permute-start(bf16[16,8320]{1,0:T(8,128)(2,1)S(1)} %pad_maximum_fusion.4), channel_id=1, source_target_pairs={{0,2},{1,3},{2,0},{3,1},{4,6},{5,7},{6,4},{7,5},{8,10},{9,11},{10,... | collective-permute-start | bytes 798728 | tf_op jit(solution)/shard_map/ppermute | solution.py:267
  17.9 12.8 %collective-permute-start.11 = (bf16[16,8320]{1,0:T(8,128)(2,1)S(1)}, bf16[16,8320]{1,0:T(8,128)(2,1)S(1)}, u32[]{:S(2)}, u32[]{:S(2)}) collective-permute-start(bf16[16,8320]{1,0:T(8,128)(2,1)S(1)} %pad_maximum_fusion.3), channel_id=1, source_target_pairs={{0,4},{1,5},{2,6},{3,7},{4,0},{5,1},{6,2},{7,3},{8,12},{9,13},{10,... | collective-permute-start | bytes 798728 | tf_op jit(solution)/shard_map/ppermute | solution.py:267
  22.0 25.1 %collective-permute-start.23 = (bf16[32,3584]{1,0:T(8,128)(2,1)S(1)}, bf16[32,3584]{1,0:T(8,128)(2,1)}, u32[]{:S(2)}, u32[]{:S(2)}) collective-permute-start(bf16[32,3584]{1,0:T(8,128)(2,1)S(1)} %collective-permute-done.22.refs_2_), channel_id=1, source_target_pairs={{0,16},{16,0},{1,17},{17,1},{2,18},{18,2},{3,19},{19,3},{4,20},{20... | collective-permute-start | bytes 688136 | tf_op jit(solution)/shard_map/ppermute | solution.py:270
  25.0 22.2 %collective-permute-start.25 = (bf16[32,3584]{1,0:T(8,128)(2,1)}, bf16[32,3584]{1,0:T(8,128)(2,1)}, u32[]{:S(2)}, u32[]{:S(2)}) collective-permute-start(bf16[32,3584]{1,0:T(8,128)(2,1)} %collective-permute-done.24.refs_4_), channel_id=1, source_target_pairs={{0,16},{16,0},{1,17},{17,1},{2,18},{18,2},{3,19},{19,3},{4,20},{20... | collective-permute-start | bytes 688136 | tf_op jit(solution)/shard_map/ppermute | solution.py:270
  30.6 2.0 %collective-permute-start.16 = (bf16[32,8320]{1,0:T(8,128)(2,1)S(1)}, bf16[32,8320]{1,0:T(8,128)(2,1)S(1)}, u32[]{:S(2)}, u32[]{:S(2)}) collective-permute-start(bf16[32,8320]{1,0:T(8,128)(2,1)S(1)} %constant_dynamic-update-slice_fusion.refs_1_), channel_id=1, source_target_pairs={{0,1},{1,0},{2,3},{3,2},{4,5},{5,4},{6,7},{7,6},{8,9},{9,8},{10,11... | collective-permute-start | bytes 1597448 | tf_op jit(solution)/shard_map/ppermute | solution.py:267
  30.8 2.6 %collective-permute-start.15 = (bf16[32,8320]{1,0:T(8,128)(2,1)S(1)}, bf16[32,8320]{1,0:T(8,128)(2,1)S(1)}, u32[]{:S(2)}, u32[]{:S(2)}) collective-permute-start(bf16[32,8320]{1,0:T(8,128)(2,1)S(1)} %pad_maximum_fusion.2.refs_0_), channel_id=1, source_target_pairs={{0,1},{1,0},{2,3},{3,2},{4,5},{5,4},{6,7},{7,6},{8,9},{9,8},{10,11... | collective-permute-start | bytes 1597448 | tf_op jit(solution)/shard_map/ppermute | solution.py:267
  34.8 7.2 %collective-permute-start.20 = (bf16[128,64]{1,0:T(8,128)(2,1)S(1)}, bf16[128,64]{1,0:T(8,128)(2,1)S(1)}, u32[]{:S(2)}, u32[]{:S(2)}) collective-permute-start(bf16[128,64]{1,0:T(8,128)(2,1)S(1)} %convolution_convert_fusion), channel_id=1, source_target_pairs={{0,2},{1,3},{2,0},{3,1},{4,6},{5,7},{6,4},{7,5},{8,10},{9,11},{10,... | collective-permute-start | bytes 49160 | tf_op jit(solution)/shard_map/ppermute | solution.py:267
  36.9 3.7 %collective-permute-start.17 = (s32[8,128]{1,0:T(8,128)S(1)}, s32[8,128]{1,0:T(8,128)S(1)}, u32[]{:S(2)}, u32[]{:S(2)}) collective-permute-start(s32[8,128]{1,0:T(8,128)S(1)} %broadcast_in_dim.29), channel_id=1, source_target_pairs={{0,16},{16,0},{1,17},{17,1},{2,18},{18,2},{3,19},{19,3},{4,20},{20... | collective-permute-start | bytes 12296 | tf_op jit(solution)/shard_map/ppermute | solution.py:270
  40.6 3.6 %collective-permute-start.21 = (bf16[128,64]{1,0:T(8,128)(2,1)S(1)}, bf16[128,64]{1,0:T(8,128)(2,1)S(1)}, u32[]{:S(2)}, u32[]{:S(2)}) collective-permute-start(bf16[128,64]{1,0:T(8,128)(2,1)S(1)} %convolution_convert_fusion), channel_id=1, source_target_pairs={{0,3},{1,2},{2,1},{3,0},{4,7},{5,6},{6,5},{7,4},{8,11},{9,10},{10,... | collective-permute-start | bytes 49160 | tf_op jit(solution)/shard_map/ppermute | solution.py:267
  42.0 2.5 %collective-permute-start.18 = (bf16[128,64]{1,0:T(8,128)(2,1)S(1)}, bf16[128,64]{1,0:T(8,128)(2,1)S(1)}, u32[]{:S(2)}, u32[]{:S(2)}) collective-permute-start(bf16[128,64]{1,0:T(8,128)(2,1)S(1)} %convolution_convert_fusion), channel_id=1, source_target_pairs={{0,1},{1,0},{2,3},{3,2},{4,5},{5,4},{6,7},{7,6},{8,9},{9,8},{10,11... | collective-permute-start | bytes 49160 | tf_op jit(solution)/shard_map/ppermute | solution.py:267
  49.1 24.3 %copy-start.5 = (bf16[128,128]{1,0:T(8,128)(2,1)S(1)}, bf16[128,128]{1,0:T(8,128)(2,1)}, u32[]{:S(2)}) copy-start(bf16[128,128]{1,0:T(8,128)(2,1)} %fusion.13) | copy-start | bytes 98308
  49.1 24.2 %collective-permute-start.26 = (bf16[64,1792]{1,0:T(8,128)(2,1)S(1)}, bf16[64,1792]{1,0:T(8,128)(2,1)S(1)}, u32[]{:S(2)}, u32[]{:S(2)}) collective-permute-start(bf16[64,1792]{1,0:T(8,128)(2,1)S(1)} %get-tuple-element.230), channel_id=1, source_target_pairs={{0,4},{1,5},{2,6},{3,7},{4,0},{5,1},{6,2},{7,3},{8,12},{9,13},{10,... | collective-permute-start | bytes 688136 | tf_op jit(solution)/shard_map/ppermute | solution.py:267
  49.7 23.7 %collective-permute-start.27 = (bf16[64,1792]{1,0:T(8,128)(2,1)S(1)}, bf16[64,1792]{1,0:T(8,128)(2,1)S(1)}, u32[]{:S(2)}, u32[]{:S(2)}) collective-permute-start(bf16[64,1792]{1,0:T(8,128)(2,1)S(1)} %get-tuple-element.231), channel_id=1, source_target_pairs={{0,8},{1,9},{2,10},{3,11},{4,12},{5,13},{6,14},{7,15},{8,0},{9,1},... | collective-permute-start | bytes 688136 | tf_op jit(solution)/shard_map/ppermute | solution.py:267
  52.2 21.1 %collective-permute-start.28 = (bf16[64,1792]{1,0:T(8,128)(2,1)S(1)}, bf16[64,1792]{1,0:T(8,128)(2,1)S(1)}, u32[]{:S(2)}, u32[]{:S(2)}) collective-permute-start(bf16[64,1792]{1,0:T(8,128)(2,1)S(1)} %get-tuple-element.232), channel_id=1, source_target_pairs={{0,12},{1,13},{2,14},{3,15},{4,8},{5,9},{6,10},{7,11},{8,4},{9,5},... | collective-permute-start | bytes 688136 | tf_op jit(solution)/shard_map/ppermute | solution.py:267
  53.6 19.8 %collective-permute-start.29 = (bf16[64,1792]{1,0:T(8,128)(2,1)S(1)}, bf16[64,1792]{1,0:T(8,128)(2,1)S(1)}, u32[]{:S(2)}, u32[]{:S(2)}) collective-permute-start(bf16[64,1792]{1,0:T(8,128)(2,1)S(1)} %get-tuple-element.233), channel_id=1, source_target_pairs={{0,2},{1,3},{2,0},{3,1},{4,6},{5,7},{6,4},{7,5},{8,10},{9,11},{10,... | collective-permute-start | bytes 688136 | tf_op jit(solution)/shard_map/ppermute | solution.py:267
  54.7 18.7 %collective-permute-start.30 = (bf16[64,1792]{1,0:T(8,128)(2,1)S(1)}, bf16[64,1792]{1,0:T(8,128)(2,1)S(1)}, u32[]{:S(2)}, u32[]{:S(2)}) collective-permute-start(bf16[64,1792]{1,0:T(8,128)(2,1)S(1)} %get-tuple-element.234), channel_id=1, source_target_pairs={{0,6},{1,7},{2,4},{3,5},{4,2},{5,3},{6,0},{7,1},{8,14},{9,15},{10,... | collective-permute-start | bytes 688136 | tf_op jit(solution)/shard_map/ppermute | solution.py:267
  (6 other events, 11.5 us)

commit v4 on v3

--- a/solution.py
+++ b/solution.py
@@ -60,34 +60,24 @@
 
 
 ANY = pl.BlockSpec(memory_space=pl.ANY)
+HBM = pl.BlockSpec(memory_space=pltpu.HBM)
 VMEM = pl.BlockSpec(memory_space=pltpu.VMEM)
 ROOMS = (64, 16, 48)
 FACTORS = (2, 3)
 ROWS = (0, 1)
-BLOCKS = PLANES + len(ROWS)
-
-
-def repack_kernel(width, u_ref, own_ref, core_ref, cross_ref, both_ref, held, in_sems, out_sems):
+
+
+def cut(u_ref, held, in_sems, out_sems, width, wanted):
     rank = u_ref.shape[0]
     half = rank // 2
-    me, y = lax.axis_index("dp"), lax.axis_index("groups")
-    z, x, c = me // 4, (me // 2) % 2, me % 2
+    z = lax.axis_index("dp") // 4
     ins, sends = [], []
-
-    def move(j, xx, cc, split, target):
-        n = len(ins)
-        at = pl.multiple_of(((lax.bitwise_xor(z, j) * 2 + xx) * 2 + cc) * width, LANES)
-        rows = pl.ds(pl.multiple_of(y * half, half), half) if split else pl.ds(0, rank)
-        here = held.at[pl.ds(0, half if split else rank), pl.ds(n * width, width)]
+    for n, (j, x, c, part, target) in enumerate(wanted):
+        at = pl.multiple_of(((lax.bitwise_xor(z, j) * 2 + x) * 2 + c) * width, LANES)
+        rows = pl.ds(0, rank) if part is None else pl.ds(pl.multiple_of(part * half, half), half)
+        here = held.at[pl.ds(0, rank if part is None else half), pl.ds(n * width, width)]
         ins.append(pltpu.make_async_copy(u_ref.at[rows, pl.ds(at, width)], here, in_sems.at[n]))
         sends.append(pltpu.make_async_copy(here, target, out_sems.at[n]))
-
-    for i, j in enumerate(FACTORS):
-        move(j, 1 - x, c, True, cross_ref.at[:, pl.ds(i * width, width)])
-        move(j, 1 - x, 1 - c, True, both_ref.at[:, pl.ds(i * width, width)])
-    for cc, ref in ((1 - c, core_ref), (c, own_ref)):
-        for i, (j, xx) in enumerate([(j, x) for j in range(PLANES)] + [(j, 1 - x) for j in ROWS]):
-            move(j, xx, cc, False, ref.at[:, pl.ds(i * width, width)])
     for copy in ins:
         copy.start()
     for copy, send in zip(ins, sends):
@@ -97,32 +87,135 @@
         send.wait()
 
 
+def position():
+    me = lax.axis_index("dp")
+    return (me // 2) % 2, me % 2
+
+
+def cross_kernel(width, u_ref, cross_ref, both_ref, *scratch):
+    (x, c), y = position(), lax.axis_index("groups")
+    wanted = []
+    for i, j in enumerate(FACTORS):
+        place = pl.ds(i * width, width)
+        wanted += [(j, 1 - x, c, y, cross_ref.at[:, place]), (j, 1 - x, 1 - c, y, both_ref.at[:, place])]
+    cut(u_ref, *scratch, width, wanted)
+
+
+def cut_cross(u, width):
+    rank = u.shape[0]
+    n = 2 * len(FACTORS)
+    split = jax.ShapeDtypeStruct((rank // 2, len(FACTORS) * width), BF16)
+    return pl.pallas_call(
+        functools.partial(cross_kernel, width),
+        out_shape=[split, split],
+        in_specs=[HBM],
+        out_specs=[ANY, ANY],
+        scratch_shapes=[
+            pltpu.VMEM((rank // 2, n * width), BF16),
+            pltpu.SemaphoreType.DMA((n,)),
+            pltpu.SemaphoreType.DMA((n,)),
+        ],
+        compiler_params=pltpu.CompilerParams(vmem_limit_bytes=61 * 1024 * 1024),
+        cost_estimate=pl.CostEstimate(flops=0, bytes_accessed=2 * rank * n * width, transcendentals=0),
+        name="cut_cross",
+    )(u)
+
+
+def repack_kernel(width, u_ref, own_rows_ref, own_ref, core_rows_ref, core_ref, *scratch):
+    x, c = position()
+    wanted = []
+    for cc, rows_ref, ref in ((1 - c, core_rows_ref, core_ref), (c, own_rows_ref, own_ref)):
+        for target, blocks in (
+            (ref, [(j, x) for j in FACTORS]),
+            (rows_ref, [(j, xx) for xx in (x, 1 - x) for j in ROWS]),
+        ):
+            for i, (j, xx) in enumerate(blocks):
+                wanted.append((j, xx, cc, None, target.at[:, pl.ds(i * width, width)]))
+    cut(u_ref, *scratch, width, wanted)
+
+
 def repack(u, width):
     rank = u.shape[0]
-    wide = jax.ShapeDtypeStruct((rank, BLOCKS * width), BF16)
-    split = jax.ShapeDtypeStruct((rank // 2, len(FACTORS) * width), BF16)
-    shapes = [wide, wide, split, split]
+    n = 2 * (len(FACTORS) + 2 * len(ROWS))
+    for_rows = jax.ShapeDtypeStruct((rank, 2 * len(ROWS) * width), BF16)
+    for_factors = jax.ShapeDtypeStruct((rank, len(FACTORS) * width), BF16)
     return pl.pallas_call(
         functools.partial(repack_kernel, width),
-        out_shape=shapes,
-        in_specs=[ANY],
-        out_specs=[ANY] * len(shapes),
+        out_shape=[for_rows, for_factors] * 2,
+        in_specs=[HBM],
+        out_specs=[ANY] * 4,
         scratch_shapes=[
-            pltpu.VMEM((rank, 16 * width), BF16),
-            pltpu.SemaphoreType.DMA((16,)),
-            pltpu.SemaphoreType.DMA((16,)),
+            pltpu.VMEM((rank, n * width), BF16),
+            pltpu.SemaphoreType.DMA((n,)),
+            pltpu.SemaphoreType.DMA((n,)),
         ],
-        compiler_params=pltpu.CompilerParams(vmem_limit_bytes=16 * 1024 * 1024),
+        compiler_params=pltpu.CompilerParams(vmem_limit_bytes=61 * 1024 * 1024),
         cost_estimate=pl.CostEstimate(flops=0, bytes_accessed=3 * u.size, transcendentals=0),
         name="repack",
     )(u)
+
+
+def low_kernel(*refs):
+    x_refs, (down_ref, table_ref, at_ref, at_column_ref), outs = refs[:4], refs[4:8], refs[8:]
+    low_ref, meta_ref, pick_ref, order_ref, rounds_ref = outs
+    depth = down_ref.shape[1]
+    x = jnp.concatenate([ref[:, :depth] for ref in x_refs], axis=0)
+    low = lax.dot_general(x, down_ref[...], (((1,), (1,)), ((), ())), preferred_element_type=F32).astype(BF16)
+    ids = jnp.concatenate([ref[:, depth:] for ref in x_refs], axis=0).astype(F32)
+    total = ids.shape[0]
+    lane = lax.broadcasted_iota(jnp.int32, ids.shape, 1).astype(F32)
+    place = lax.broadcasted_iota(jnp.int32, ids.shape, 0).astype(F32)
+    table = jnp.broadcast_to(table_ref[...], ids.shape).astype(F32)
+    slots = jnp.broadcast_to(jnp.sum(jnp.where(ids == lane, table, 0.0), axis=1, keepdims=True), (total, total))
+    slots_row = slots.T
+    planes, planes_row = jnp.floor(slots * 0.25), jnp.floor(slots_row * 0.25)
+    at = jnp.broadcast_to(at_ref[...], ids.shape).astype(F32)
+    at_column = jnp.broadcast_to(at_column_ref[...], ids.shape).astype(F32)
+    same = planes == planes_row
+    ranks_row = jnp.sum(jnp.where(same & (at_column < at), 1.0, 0.0), axis=0, keepdims=True)
+    ranks = jnp.sum(jnp.where(same & (at < at_column), 1.0, 0.0), axis=1, keepdims=True)
+    me = lax.axis_index("dp")
+    mine = jnp.where((slots_row == me.astype(F32)) & (ranks_row == place), 1.0, 0.0).astype(BF16)
+    low_ref[...] = jnp.dot(mine, low, preferred_element_type=F32).astype(BF16)
+    meta_ref[0:1, :] = slots_row[0:1, :].astype(jnp.int32)
+    meta_ref[1:2, :] = ranks_row.astype(jnp.int32)
+    order_ref[...] = jnp.where(at == place, 1.0, 0.0).astype(BF16)
+    room = ROOMS[0]
+    wide = lax.broadcasted_iota(jnp.int32, pick_ref.shape, 1)
+    block = wide // room
+    distance = jnp.where(block < PLANES, block, block - PLANES)
+    wanted = lax.bitwise_xor(distance, jnp.broadcast_to(me // 4, distance.shape)).astype(F32)
+    found = (planes[:, :1] == wanted) & (ranks == (wide % room).astype(F32))
+    pick_ref[...] = jnp.where(found, 1.0, 0.0).astype(BF16)
+    most = jnp.max(ranks_row)
+    rounds_ref[0] = (most >= room).astype(jnp.int32) + (most >= room + ROOMS[1]).astype(jnp.int32)
+
+
+def low_rows(x_parts, down, table, order_of):
+    total = order_of.shape[0]
+    rank = down.shape[0]
+    return pl.pallas_call(
+        low_kernel,
+        out_shape=[
+            jax.ShapeDtypeStruct((total, rank), BF16),
+            jax.ShapeDtypeStruct((2, total), jnp.int32),
+            jax.ShapeDtypeStruct((total, (PLANES + len(ROWS)) * ROOMS[0]), BF16),
+            jax.ShapeDtypeStruct((total, total), BF16),
+            jax.ShapeDtypeStruct((1,), jnp.int32),
+        ],
+        in_specs=[VMEM] * 8,
+        out_specs=[VMEM] * 4 + [pl.BlockSpec(memory_space=pltpu.SMEM)],
+        compiler_params=pltpu.CompilerParams(vmem_limit_bytes=16 * 1024 * 1024),
+        cost_estimate=pl.CostEstimate(flops=0, bytes_accessed=60 * 1024 * 1024, transcendentals=0),
+        name="low_rows",
+    )(*x_parts, down, table, order_of[None, :], order_of[:, None])
 
 
 def delta_kernel(plan, width, e_ref, *refs):
     parts, outs = refs[: len(refs) - len(plan)], refs[len(refs) - len(plan) :]
     for pieces, out in zip(plan, outs):
         stacked = jnp.concatenate(
-            [parts[n][:rows, i * width : (i + 1) * width] for n, i, rows in pieces], axis=0
+            [parts[n][at : at + rows, i * width : (i + 1) * width] for n, i, at, rows in pieces], axis=0
         )
         out[...] = jnp.dot(e_ref[:, : stacked.shape[0]], stacked, preferred_element_type=F32).astype(BF16)
 
@@ -135,7 +228,7 @@
         out_shape=[jax.ShapeDtypeStruct((rows, width), BF16)] * n,
         in_specs=[VMEM] * (1 + len(parts)),
         out_specs=[VMEM] * n,
-        compiler_params=pltpu.CompilerParams(vmem_limit_bytes=16 * 1024 * 1024),
+        compiler_params=pltpu.CompilerParams(vmem_limit_bytes=8 * 1024 * 1024),
         cost_estimate=pl.CostEstimate(
             flops=2 * rows * e.shape[1] * width * n,
             bytes_accessed=2 * n * width * (rows + e.shape[1]),
@@ -203,7 +296,7 @@
     return pl.pallas_call(
         functools.partial(base_kernel, first, steps, rows, bool(sums)),
         out_shape=[shape, shape],
-        in_specs=[ANY] * (len(x_parts) + 2) + [VMEM] * len(sums),
+        in_specs=[ANY] * len(x_parts) + [HBM] * 2 + [VMEM] * len(sums),
         out_specs=[VMEM, VMEM],
         scratch_shapes=[
             pltpu.VMEM((total, steps * BLOCK), BF16),
@@ -213,7 +306,7 @@
             pltpu.SemaphoreType.DMA((SLOTS,)),
             pltpu.SemaphoreType.DMA((SLOTS,)),
         ],
-        compiler_params=pltpu.CompilerParams(vmem_limit_bytes=32 * 1024 * 1024),
+        compiler_params=pltpu.CompilerParams(vmem_limit_bytes=30 * 1024 * 1024),
         cost_estimate=pl.CostEstimate(
             flops=4 * total * steps * BLOCK * width, bytes_accessed=4 * steps * BLOCK * width, transcendentals=0
         ),
@@ -223,8 +316,7 @@
 
 def finish_kernel(gate_ref, up_ref, pick_ref, order_ref, *refs):
     stacked = jnp.concatenate([ref[...] for ref in refs[:-1]], axis=0)
-    delta = jnp.dot(pick_ref[...], stacked, preferred_element_type=F32)
-    gate = gate_ref[...] + delta
+    gate = gate_ref[...] + jnp.dot(pick_ref[...], stacked, preferred_element_type=F32)
     hidden = (gate / (1.0 + jnp.exp(-gate)) * up_ref[...]).astype(BF16)
     refs[-1][...] = jnp.dot(order_ref[...], hidden, preferred_element_type=F32).astype(BF16)
 
@@ -272,80 +364,77 @@
     ids = jnp.broadcast_to(token_adapter_index.astype(BF16), (own_rows, LANES))
     packed = jnp.concatenate([tokens, ids], axis=1)
     second, third = swap(packed, 8), swap(packed, 12)
+    cross, both = cut_cross(adapter_up_factor[0], width)
+    cross, both = swap(cross, 2), swap(both, 3)
     pair = jnp.concatenate([packed, swap(packed, 2)], axis=0)
+    remote = jnp.concatenate([second, third], axis=0)
+    own_chip, own_plane, core_chip, core_plane = repack(adapter_up_factor[0], width)
+    core_chip, core_plane = swap(core_chip, 1), swap(core_plane, 1)
+    pair, remote, down, core_chip, core_plane = lax.optimization_barrier(
+        (pair, remote, adapter_down_factor[0], core_chip, core_plane)
+    )
     close = jnp.concatenate([pair, swap(pair, 4)], axis=0)
-    remote = jnp.concatenate([second, third], axis=0)
     remote = jnp.concatenate([remote, swap(remote, 2)], axis=0)
+    close, cross, both = lax.optimization_barrier((close, cross, both))
     x_parts = (close, remote, swap(close, 1), swap(remote, 1))
     distances = [0, 2, 4, 6, 8, 12, 10, 14]
     distances = distances + [k + 1 for k in distances]
 
-    own, core, cross, both = repack(adapter_up_factor[0], width)
-    core = swap(core, 1)
-    cross, both = swap(cross, 2), swap(both, 3)
-    cross_parts = (cross, other(cross), both, other(both))
+    crossed = jnp.concatenate([cross, both], axis=0)
+    cross_parts = (crossed, other(crossed))
     half = rank // 2
 
     place = jnp.arange(total, dtype=jnp.int32)
     order_of = (jnp.repeat(jnp.array(distances, jnp.int32), own_rows) ^ me) * own_rows + place % own_rows
-    all_ids = jnp.concatenate([v[:, depth] for v in x_parts]).astype(jnp.int32)
-    adapters = jnp.arange(count, dtype=jnp.int32)
-    slots = jnp.sum(jnp.where(all_ids[:, None] == adapters[None, :], adapter_slot_index[None, :], 0), 1)
-    planes = slots // 4
-    before = (planes[None, :] == planes[:, None]) & (order_of[None, :] < order_of[:, None])
-    ranks = jnp.sum(before.astype(jnp.int32), 1)
-
-    low = jnp.concatenate(
-        [jnp.dot(v[:, :depth], adapter_down_factor[0], preferred_element_type=F32) for v in x_parts], axis=0
-    ).astype(BF16)
-    mine = ((slots == me)[None, :] & (ranks[None, :] == place[:, None])).astype(BF16)
-    low = jnp.dot(mine, low, preferred_element_type=F32).astype(BF16)
-    low, x_parts, slots, ranks = lax.optimization_barrier((low, x_parts, slots, ranks))
+    table = jnp.pad(adapter_slot_index, (0, LANES - count))[None, :]
+    low, meta, first, order, rounds = low_rows(x_parts, down.T, table, order_of)
+    slots, ranks = meta[0], meta[1]
 
     def turned(v):
         return jnp.where(y == 0, v, jnp.concatenate([v[:, half:], v[:, :half]], axis=1))
 
+    chip_plan = tuple(((0, i, 0, rank), (1, i, 0, rank)) for i in range(2 * len(ROWS)))
+    plane_plan = tuple(
+        ((0, i, 0, rank), (1, i, 0, rank)) + tuple((n, i, at, half) for at in (0, half) for n in (2, 3))
+        for i in range(len(FACTORS))
+    )
+
+    def chip_rows(e):
+        return delta_rows(e, (own_chip, core_chip), chip_plan, width)
+
+    def plane_rows(e):
+        return delta_rows(e, (own_plane, core_plane, *cross_parts), plane_plan, width)
+
+    def arrived(chip, plane):
+        here, first, here_cross, first_cross = chip
+        second, third = plane
+        return [here, swap(first, 4), swap(second, 8), swap(third, 12), swap(here_cross, 2), swap(first_cross, 6)]
+
+    cross_low, both_low = swap(low, 2), swap(low, 3)
     chip = jnp.concatenate([low, swap(low, 1)], axis=1)
-    plane = jnp.concatenate([chip, turned(swap(low, 2)), turned(swap(low, 3))], axis=1)
-    chip_plan = tuple(((0, i, rank), (1, i, rank)) for i in (0, 1, PLANES, PLANES + 1))
-    plane_plan = tuple(
-        ((0, j, rank), (1, j, rank)) + tuple((n, i, half) for n in (2, 3, 4, 5)) for i, j in enumerate(FACTORS)
-    )
-
-    def sent(start, room):
-        at = slice(start, start + room)
-        here, first, here_cross, first_cross = delta_rows(chip[at], (own, core), chip_plan, width)
-        second, third = delta_rows(plane[at], (own, core, *cross_parts), plane_plan, width)
-        return here, first, second, third, here_cross, first_cross
-
-    def arrived(rows):
-        return [rows[0]] + [swap(v, k) for v, k in zip(rows[1:], (4, 8, 12, 2, 6))]
-
-    rows, x_parts = lax.optimization_barrier((sent(0, ROOMS[0]), x_parts))
-    rows = arrived(rows)
+    by_chip = chip_rows(chip[: ROOMS[0]])
+    by_chip, cross_low, both_low = lax.optimization_barrier((by_chip, cross_low, both_low))
+    plane = jnp.concatenate([chip, turned(cross_low), turned(both_low)], axis=1)
+    by_plane = plane_rows(plane[: ROOMS[0]])
+    by_plane, x_parts, slots, ranks = lax.optimization_barrier((by_plane, x_parts, slots, ranks))
+    rows = arrived(by_chip, by_plane)
     gate, up = base(x_parts, gate_matrix, up_matrix, 0, depth // BLOCK)
-
-    order = (order_of[None, :] == place[:, None]).astype(BF16)
-    most = jnp.max(ranks) + 1
-    most = jnp.maximum(most, jnp.max(other(jnp.broadcast_to(most, (8, LANES)))))
-    branch = (most > ROOMS[0]).astype(jnp.int32) + (most > ROOMS[0] + ROOMS[1]).astype(jnp.int32)
 
     def picked(start, room):
         at = jnp.where((ranks >= start) & (ranks < start + room), ((slots // 4) ^ z) * room + ranks - start, -1)
         pick = (at[:, None] == jnp.arange(PLANES * room, dtype=jnp.int32)[None, :]).astype(BF16)
         return jnp.concatenate([pick, pick[:, : len(ROWS) * room]], axis=1)
 
-    first = picked(0, ROOMS[0])
-
     def short():
         return finish(gate, up, first, order, rows)
 
     def more(room):
-        rest = arrived(sent(ROOMS[0], room))
+        at = slice(ROOMS[0], ROOMS[0] + room)
+        rest = arrived(chip_rows(chip[at]), plane_rows(plane[at]))
         pick = jnp.concatenate([first, picked(ROOMS[0], room)], axis=1)
         return finish(gate, up, pick, order, rows + rest)
 
-    return lax.switch(branch, (short, lambda: more(ROOMS[1]), lambda: more(ROOMS[1] + ROOMS[2])))
+    return lax.switch(rounds[0], (short, lambda: more(ROOMS[1]), lambda: more(ROOMS[1] + ROOMS[2])))
 
 
 def solution(mesh):

time: 77.1 us -> 67.7 us (0.88)
  local copies, waits for them, and re-layouts: 4.96 us -> 2.29 us
  starting transfers between devices: 24.9 us -> 22.9 us
  matrix products: 1.76 us -> 0 us
  waiting for transfers between devices: 11.8 us -> 11 us
  other arithmetic: 4.7 us -> 3.92 us
    pallas_call x2, Pallas kernels: 4.23 us -> 0.83 us  [delta_rows(): pl.pallas_call(functools.partial(delta_kernel, plan, width), out_shape=[j...]
    unnamed x20 -> x16, local copies, waits for them, and re-layouts: 4.09 us -> 0.82 us
    ppermute x3 -> x1, starting transfers between devices: 4.62 us -> 1.58 us  [other(): return lax.ppermute(value, 'groups', [(0, 1), (1, 0)])]
    pallas_call x1 -> x3, Pallas kernels: 2.65 us -> 5.5 us  [the longest x1 2.45 us: repack(): pl.pallas_call(functools.partial(repack_kernel, width), out_shape=[for_ro...]
    dot_general x5 -> x0, matrix products: 1.76 us -> none  [the longest x4 1.61 us: plane_shards(): jnp.dot(v[:, :depth], adapter_down_factor[0], preferred_element_type=F32)]
    ppermute x3 -> x1, waiting for transfers between devices: 2.08 us -> 1.01 us  [other(): return lax.ppermute(value, 'groups', [(0, 1), (1, 0)])]
    ppermute x18 -> x19, starting transfers between devices: 20.3 us -> 21.3 us  [swap(): return lax.ppermute(value, 'dp', [(d, d ^ k) for d in range(count)])]
    concatenate x0 -> x1, local copies, waits for them, and re-layouts: none -> 0.96 us  [plane_shards(): crossed = jnp.concatenate([cross, both], axis=0)]
  transfers between devices with their start and end apart: 21 -> 20, of which waited for: 9 -> 7; matrix products, arithmetic and copies ran while one was open for 7% -> 6% of each run, Pallas kernels for 31% -> 37%
where the time goes in v4:
time: 67.7 us; the launch traced here: 67.5 us
  Pallas kernels  26.4 us (39%)
  starting transfers between devices  22.9 us (34%)
  waiting for transfers between devices  11 us (16%)
  other arithmetic  3.92 us (6%)
  local copies, waits for them, and re-layouts  2.29 us (3%)
  between operations  0.95 us (1%)
    ppermute x19, starting transfers between devices, swap(): return lax.ppermute(value, 'dp', [(d, d ^ k) for d in range(count)])  21.3 us
    pallas_call x1, Pallas kernels, base(): pl.pallas_call(functools.partial(base_kernel, first, steps, rows, bool(su...  18.7 us
    ppermute x19, waiting for transfers between devices, swap(): return lax.ppermute(value, 'dp', [(d, d ^ k) for d in range(count)])  10 us
    pallas_call x1, Pallas kernels, repack(): pl.pallas_call(functools.partial(repack_kernel, width), out_shape=[for_ro...  2.45 us
    pallas_call x1, Pallas kernels, cut_cross(): pl.pallas_call(functools.partial(cross_kernel, width), out_shape=[split,...  1.83 us
    ppermute x1, starting transfers between devices, other(): return lax.ppermute(value, 'groups', [(0, 1), (1, 0)])  1.58 us
    pallas_call x1, Pallas kernels, finish(): pl.pallas_call(finish_kernel, out_shape=jax.ShapeDtypeStruct((total, widt...  1.41 us
  transfers between devices with their start and end apart: 20, of which 7 were waited for; matrix products, arithmetic and copies ran while one was open for 6% of the time, Pallas kernels for 37%

profile of v4, /device:TPU:0, one launch (start us, length us, event | category | flops | bytes accessed | tf_op | source)
XLA Modules:
  0.0 67.5 jit_solution(9823621170165448406)
XLA Ops:
  1.7 4.1 %collective-permute-start.11 = (bf16[8,8320]{1,0:T(8,128)(2,1)S(1)}, bf16[8,8320]{1,0:T(8,128)(2,1)}, u32[]{:S(2)}, u32[]{:S(2)}) collective-permute-start(bf16[8,8320]{1,0:T(8,128)(2,1)S(1)} %pad_maximum_fusion.5), channel_id=1, source_target_pairs={{0,8},{1,9},{2,10},{3,11},{4,12},{5,13},{6,14},{7,15},{8,0},{9,1},... | collective-permute-start | bytes 399368 | tf_op jit(solution)/shard_map/ppermute | solution.py:359
  5.8 1.3 %collective-permute-start.12 = (bf16[8,8320]{1,0:T(8,128)(2,1)S(1)}, bf16[8,8320]{1,0:T(8,128)(2,1)}, u32[]{:S(2)}, u32[]{:S(2)}) collective-permute-start(bf16[8,8320]{1,0:T(8,128)(2,1)S(1)} %pad_maximum_fusion.5), channel_id=1, source_target_pairs={{0,12},{1,13},{2,14},{3,15},{4,8},{5,9},{6,10},{7,11},{8,4},{9,5},... | collective-permute-start | bytes 399368 | tf_op jit(solution)/shard_map/ppermute | solution.py:359
  7.1 1.5 %collective-permute-start.10 = (bf16[8,8320]{1,0:T(8,128)(2,1)S(1)}, bf16[8,8320]{1,0:T(8,128)(2,1)}, u32[]{:S(2)}, u32[]{:S(2)}) collective-permute-start(bf16[8,8320]{1,0:T(8,128)(2,1)S(1)} %pad_maximum_fusion.5), channel_id=1, source_target_pairs={{0,2},{1,3},{2,0},{3,1},{4,6},{5,7},{6,4},{7,5},{8,10},{9,11},{10,... | collective-permute-start | bytes 399368 | tf_op jit(solution)/shard_map/ppermute | solution.py:359
  8.6 1.8 %cut_cross.1 = (bf16[32,3584]{1,0:T(8,128)(2,1)}, bf16[32,3584]{1,0:T(8,128)(2,1)}) custom-call(bf16[64,28672]{1,0:T(8,128)(2,1)} %bitcast.14), custom_call_target="tpu_custom_call" | custom-call | bytes 917504 | tf_op jit(solution)/shard_map/cut_cross/pallas_call | solution.py:108
  11.4 2.4 %repack.1 = (bf16[64,7168]{1,0:T(8,128)(2,1)S(1)}, bf16[64,3584]{1,0:T(8,128)(2,1)S(1)}, bf16[64,7168]{1,0:T(8,128)(2,1)}, bf16[64,3584]{1,0:T(8,128)(2,1)}) custom-call(bf16[64,28672]{1,0:T(8,128)(2,1)} %bitcast.15), custom_call_target="tpu_custom_call" | custom-call | bytes 5505024 | tf_op jit(solution)/shard_map/repack/pallas_call | solution.py:142
  13.9 1.7 %collective-permute-start.14 = (bf16[64,3584]{1,0:T(8,128)(2,1)}, bf16[64,3584]{1,0:T(8,128)(2,1)S(1)}, u32[]{:S(2)}, u32[]{:S(2)}) collective-permute-start(bf16[64,3584]{1,0:T(8,128)(2,1)} %get-tuple-element.279), channel_id=1, source_target_pairs={{0,1},{1,0},{2,3},{3,2},{4,5},{5,4},{6,7},{7,6},{8,9},{9,8},{10,11... | collective-permute-start | bytes 1376264 | tf_op jit(solution)/shard_map/ppermute | solution.py:359
  15.5 0.9 %pad_maximum_fusion.3 = bf16[16,8320]{1,0:T(8,128)(2,1)S(1)} fusion(bf16[8,8320]{1,0:T(8,128)(2,1)} %collective-permute-done.10, bf16[8,128]{1,0:T(8,128)(2,1)S(1)} %broadcast_in_dim.14, bf16[8,8192]{1,0:T(8,128)(2,1)S(1)} %copy-done.17), kind=kLoop, calls=%fused_computation.17 | loop fusion | flops 798720 | bytes 532480 | tf_op jit(solution)/shard_map/concatenate | solution.py:369
  16.6 1.0 %pad_maximum_fusion.4 = bf16[16,8320]{1,0:T(8,128)(2,1)S(1)} fusion(bf16[8,8320]{1,0:T(8,128)(2,1)} %collective-permute-done.12, bf16[8,8320]{1,0:T(8,128)(2,1)} %collective-permute-done.11), kind=kLoop, calls=%fused_computation.18 | loop fusion | flops 532480 | bytes 532480 | tf_op jit(solution)/shard_map/concatenate | solution.py:370
  17.6 1.6 %collective-permute-done.13.refs_1_ = bf16[64,7168]{1,0:T(8,128)(2,1)S(1)} collective-permute-done((bf16[64,7168]{1,0:T(8,128)(2,1)}, bf16[64,7168]{1,0:T(8,128)(2,1)S(1)}, u32[]{:S(2)}, u32[]{:S(2)}) %collective-permute-start.13) | collective-permute-done | bytes 917536 | tf_op jit(solution)/shard_map/ppermute | solution.py:359
  19.7 1.5 %collective-permute-start.18 = (bf16[16,8320]{1,0:T(8,128)(2,1)S(1)}, bf16[16,8320]{1,0:T(8,128)(2,1)S(1)}, u32[]{:S(2)}, u32[]{:S(2)}) collective-permute-start(bf16[16,8320]{1,0:T(8,128)(2,1)S(1)} %pad_maximum_fusion.4), channel_id=1, source_target_pairs={{0,2},{1,3},{2,0},{3,1},{4,6},{5,7},{6,4},{7,5},{8,10},{9,11},{10,... | collective-permute-start | bytes 798728 | tf_op jit(solution)/shard_map/ppermute | solution.py:359
  21.2 6.5 %collective-permute-done.15 = bf16[16,8320]{1,0:T(8,128)(2,1)S(1)} collective-permute-done((bf16[16,8320]{1,0:T(8,128)(2,1)S(1)}, bf16[16,8320]{1,0:T(8,128)(2,1)S(1)}, u32[]{:S(2)}, u32[]{:S(2)}) %collective-permute-start.15) | collective-permute-done | bytes 266272 | tf_op jit(solution)/shard_map/ppermute | solution.py:359
  28.5 1.0 %constant_dynamic-update-slice_fusion.2.refs_2_ = bf16[64,3584]{1,0:T(8,128)(2,1)S(1)} fusion(bf16[64,3584]{1,0:T(8,128)(2,1)S(1)} %constant_dynamic-update-slice_fusion.3, bf16[32,3584]{1,0:T(8,128)(2,1)} %collective-permute-done.17), kind=kLoop, calls=%fused_computation.35 | loop fusion | bytes 458752 | tf_op jit(solution)/shard_map/concatenate | solution.py:383
  29.5 1.6 %collective-permute-start.24 = (bf16[64,3584]{1,0:T(8,128)(2,1)S(1)}, bf16[64,3584]{1,0:T(8,128)(2,1)S(1)}, u32[]{:S(2)}, u32[]{:S(2)}) collective-permute-start(bf16[64,3584]{1,0:T(8,128)(2,1)S(1)} %constant_dynamic-update-slice_fusion.2.refs_2_), channel_id=1, source_target_pairs={{0,16},{16,0},{1,17},{17,1},{2,18},{18,2},{3,19},{19,3},{4,20},{20... | collective-permute-start | bytes 1376264 | tf_op jit(solution)/shard_map/ppermute | solution.py:362
  31.0 1.2 %low_rows.1 = (bf16[128,64]{1,0:T(8,128)(2,1)S(1)}, s32[2,128]{1,0:T(2,128)S(1)}, bf16[128,384]{1,0:T(8,128)(2,1)S(1)}, bf16[128,128]{1,0:T(8,128)(2,1)S(1)}, s32[1]{0:T(128)}) custom-call(bf16[32,8320]{1,0:T(8,128)(2,1)S(1)} %pad_maximum_fusion.2.refs_0_, bf16[32,8320]{1,0:T(8,128)(2,1)S(1)} %constant_dynamic-update-slice_fusion.refs_1_, ...), custom_call_target="tpu_custom_call" | custom-call | bytes 62914560 | tf_op jit(solution)/shard_map/low_rows/pallas_call | solution.py:197
  36.0 1.1 %collective-permute-done.22 = bf16[128,64]{1,0:T(8,128)(2,1)S(1)} collective-permute-done((bf16[128,64]{1,0:T(8,128)(2,1)S(1)}, bf16[128,64]{1,0:T(8,128)(2,1)S(1)}, u32[]{:S(2)}, u32[]{:S(2)}) %collective-permute-start.22) | collective-permute-done | bytes 16416 | tf_op jit(solution)/shard_map/ppermute | solution.py:359
  37.5 1.5 %collective-permute-start.25 = (bf16[64,1792]{1,0:T(8,128)(2,1)S(1)}, bf16[64,1792]{1,0:T(8,128)(2,1)S(1)}, u32[]{:S(2)}, u32[]{:S(2)}) collective-permute-start(bf16[64,1792]{1,0:T(8,128)(2,1)S(1)} %get-tuple-element.312), channel_id=1, source_target_pairs={{0,4},{1,5},{2,6},{3,7},{4,0},{5,1},{6,2},{7,3},{8,12},{9,13},{10,... | collective-permute-start | bytes 688136 | tf_op jit(solution)/shard_map/ppermute | solution.py:359
  39.0 1.0 %collective-permute-start.28 = (bf16[64,1792]{1,0:T(8,128)(2,1)S(1)}, bf16[64,1792]{1,0:T(8,128)(2,1)S(1)}, u32[]{:S(2)}, u32[]{:S(2)}) collective-permute-start(bf16[64,1792]{1,0:T(8,128)(2,1)S(1)} %get-tuple-element.315), channel_id=1, source_target_pairs={{0,2},{1,3},{2,0},{3,1},{4,6},{5,7},{6,4},{7,5},{8,10},{9,11},{10,... | collective-permute-start | bytes 688136 | tf_op jit(solution)/shard_map/ppermute | solution.py:359
  39.9 1.1 %collective-permute-start.29 = (bf16[64,1792]{1,0:T(8,128)(2,1)S(1)}, bf16[64,1792]{1,0:T(8,128)(2,1)S(1)}, u32[]{:S(2)}, u32[]{:S(2)}) collective-permute-start(bf16[64,1792]{1,0:T(8,128)(2,1)S(1)} %get-tuple-element.316), channel_id=1, source_target_pairs={{0,6},{1,7},{2,4},{3,5},{4,2},{5,3},{6,0},{7,1},{8,14},{9,15},{10,... | collective-permute-start | bytes 688136 | tf_op jit(solution)/shard_map/ppermute | solution.py:359
  41.0 1.0 %collective-permute-done.24.refs_3_ = bf16[64,3584]{1,0:T(8,128)(2,1)S(1)} collective-permute-done((bf16[64,3584]{1,0:T(8,128)(2,1)S(1)}, bf16[64,3584]{1,0:T(8,128)(2,1)S(1)}, u32[]{:S(2)}, u32[]{:S(2)}) %collective-permute-start.24) | collective-permute-done | bytes 458784 | tf_op jit(solution)/shard_map/ppermute | solution.py:362
  42.5 2.6 %collective-permute-start.26 = (bf16[64,1792]{1,0:T(8,128)(2,1)S(1)}, bf16[64,1792]{1,0:T(8,128)(2,1)S(1)}, u32[]{:S(2)}, u32[]{:S(2)}) collective-permute-start(bf16[64,1792]{1,0:T(8,128)(2,1)S(1)} %get-tuple-element.313), channel_id=1, source_target_pairs={{0,8},{1,9},{2,10},{3,11},{4,12},{5,13},{6,14},{7,15},{8,0},{9,1},... | collective-permute-start | bytes 688136 | tf_op jit(solution)/shard_map/ppermute | solution.py:359
  45.1 1.3 %collective-permute-start.27 = (bf16[64,1792]{1,0:T(8,128)(2,1)S(1)}, bf16[64,1792]{1,0:T(8,128)(2,1)S(1)}, u32[]{:S(2)}, u32[]{:S(2)}) collective-permute-start(bf16[64,1792]{1,0:T(8,128)(2,1)S(1)} %get-tuple-element.314), channel_id=1, source_target_pairs={{0,12},{1,13},{2,14},{3,15},{4,8},{5,9},{6,10},{7,11},{8,4},{9,5},... | collective-permute-start | bytes 688136 | tf_op jit(solution)/shard_map/ppermute | solution.py:359
  46.4 18.7 %base.1 = (f32[128,1792]{1,0:T(8,128)S(1)}, f32[128,1792]{1,0:T(8,128)S(1)}) custom-call(bf16[32,8320]{1,0:T(8,128)(2,1)S(1)} %pad_maximum_fusion.2.refs_0_, bf16[32,8320]{1,0:T(8,128)(2,1)S(1)} %constant_dynamic-update-slice_fusion.refs_1_, bf16[32,8320]{1,0:T(8,128)(2,1)S(1)} %collective-permute-done.19.refs_2_, ...), custom_call_target="tpu_custom_call" | custom-call | flops 7516192768 | bytes 58720256 | tf_op jit(solution)/shard_map/base/pallas_call | solution.py:296
  65.2 1.4 %conditional.1 = (bf16[128,1792]{1,0:T(8,128)(2,1)S(1)}) conditional(s32[]{:T(128)} %bitcast.5, (f32[128,1792]{1,0:T(8,128)S(1)}, f32[128,1792]{1,0:T(8,128)S(1)}, bf16[128,384]{1,0:T(8,128)(2,1)S(1)}, bf16[128,128]{1,0:T(8,128)(2,1)S(1)}, bf16[64,1792]{1,0:T(8,128)(2,1)S(1)}, /*index=5*/bf16[64,1792]{1,0:T(8,128)(2,1)S(1)}, ...), branch_computations={%region_0.1_spmd, %region_1.2_spmd, %region_2.3_spmd} | conditional | flops 235539344 | bytes 26905190 | solution.py:437
  65.3 1.4 %finish.3 = bf16[128,1792]{1,0:T(8,128)(2,1)S(1)} custom-call(f32[128,1792]{1,0:T(8,128)S(1)} %get-tuple-element.171.gate_ref, f32[128,1792]{1,0:T(8,128)S(1)} %get-tuple-element.172.up_ref, bf16[128,384]{1,0:T(8,128)(2,1)S(1)} %get-tuple-element.173.pick_ref, bf16[128,128]{1,0:T(8,128)(2,1)S(1)} %get-tuple-element.174.order_ref, ...), custom_call_target="tpu_custom_call" | custom-call | bytes 3670016 | tf_op jit(solution)/shard_map/cond/branch_0_fun/finish/pallas_call | solution.py:329
  (63 shorter events, 8.7 us)
Async XLA Ops:
  0.0 11.1 %copy-start.21 = (s32[16]{0:T(128)S(1)}, s32[16]{0:T(128)}, u32[]{:S(2)}) copy-start(s32[16]{0:T(128)} %constant.104.clone) | copy-start | bytes 196
  1.7 14.8 %collective-permute-start.11 = (bf16[8,8320]{1,0:T(8,128)(2,1)S(1)}, bf16[8,8320]{1,0:T(8,128)(2,1)}, u32[]{:S(2)}, u32[]{:S(2)}) collective-permute-start(bf16[8,8320]{1,0:T(8,128)(2,1)S(1)} %pad_maximum_fusion.5), channel_id=1, source_target_pairs={{0,8},{1,9},{2,10},{3,11},{4,12},{5,13},{6,14},{7,15},{8,0},{9,1},... | collective-permute-start | bytes 399368 | tf_op jit(solution)/shard_map/ppermute | solution.py:359
  5.8 10.8 %collective-permute-start.12 = (bf16[8,8320]{1,0:T(8,128)(2,1)S(1)}, bf16[8,8320]{1,0:T(8,128)(2,1)}, u32[]{:S(2)}, u32[]{:S(2)}) collective-permute-start(bf16[8,8320]{1,0:T(8,128)(2,1)S(1)} %pad_maximum_fusion.5), channel_id=1, source_target_pairs={{0,12},{1,13},{2,14},{3,15},{4,8},{5,9},{6,10},{7,11},{8,4},{9,5},... | collective-permute-start | bytes 399368 | tf_op jit(solution)/shard_map/ppermute | solution.py:359
  7.1 6.7 %collective-permute-start.10 = (bf16[8,8320]{1,0:T(8,128)(2,1)S(1)}, bf16[8,8320]{1,0:T(8,128)(2,1)}, u32[]{:S(2)}, u32[]{:S(2)}) collective-permute-start(bf16[8,8320]{1,0:T(8,128)(2,1)S(1)} %pad_maximum_fusion.5), channel_id=1, source_target_pairs={{0,2},{1,3},{2,0},{3,1},{4,6},{5,7},{6,4},{7,5},{8,10},{9,11},{10,... | collective-permute-start | bytes 399368 | tf_op jit(solution)/shard_map/ppermute | solution.py:359
  10.5 17.2 %collective-permute-start.16 = (bf16[32,3584]{1,0:T(8,128)(2,1)}, bf16[32,3584]{1,0:T(8,128)(2,1)S(1)}, u32[]{:S(2)}, u32[]{:S(2)}) collective-permute-start(bf16[32,3584]{1,0:T(8,128)(2,1)} %get-tuple-element.281), channel_id=1, source_target_pairs={{0,2},{1,3},{2,0},{3,1},{4,6},{5,7},{6,4},{7,5},{8,10},{9,11},{10,... | collective-permute-start | bytes 688136 | tf_op jit(solution)/shard_map/ppermute | solution.py:359
  11.1 16.7 %collective-permute-start.17 = (bf16[32,3584]{1,0:T(8,128)(2,1)}, bf16[32,3584]{1,0:T(8,128)(2,1)}, u32[]{:S(2)}, u32[]{:S(2)}) collective-permute-start(bf16[32,3584]{1,0:T(8,128)(2,1)} %get-tuple-element.282), channel_id=1, source_target_pairs={{0,3},{1,2},{2,1},{3,0},{4,7},{5,6},{6,5},{7,4},{8,11},{9,10},{10,... | collective-permute-start | bytes 688136 | tf_op jit(solution)/shard_map/ppermute | solution.py:359
  11.3 19.7 %copy-start = (bf16[1,8192,64]{1,2,0:T(8,128)(2,1)S(1)}, bf16[1,8192,64]{1,2,0:T(8,128)(2,1)}, u32[]{:S(2)}) copy-start(bf16[1,8192,64]{1,2,0:T(8,128)(2,1)} %param.16) | copy-start | bytes 3145732
  13.8 28.2 %copy-start.3 = (bf16[64,3584]{1,0:T(8,128)(2,1)}, bf16[64,3584]{1,0:T(8,128)(2,1)S(1)}, u32[]{:S(2)}) copy-start(bf16[64,3584]{1,0:T(8,128)(2,1)S(1)} %get-tuple-element.296.refs_0_) | copy-start | bytes 1376260
  13.9 3.7 %collective-permute-start.14 = (bf16[64,3584]{1,0:T(8,128)(2,1)}, bf16[64,3584]{1,0:T(8,128)(2,1)S(1)}, u32[]{:S(2)}, u32[]{:S(2)}) collective-permute-start(bf16[64,3584]{1,0:T(8,128)(2,1)} %get-tuple-element.279), channel_id=1, source_target_pairs={{0,1},{1,0},{2,3},{3,2},{4,5},{5,4},{6,7},{7,6},{8,9},{9,8},{10,11... | collective-permute-start | bytes 1376264 | tf_op jit(solution)/shard_map/ppermute | solution.py:359
  16.5 2.7 %collective-permute-start.13 = (bf16[64,7168]{1,0:T(8,128)(2,1)}, bf16[64,7168]{1,0:T(8,128)(2,1)S(1)}, u32[]{:S(2)}, u32[]{:S(2)}) collective-permute-start(bf16[64,7168]{1,0:T(8,128)(2,1)} %get-tuple-element.278), channel_id=1, source_target_pairs={{0,1},{1,0},{2,3},{3,2},{4,5},{5,4},{6,7},{7,6},{8,9},{9,8},{10,11... | collective-permute-start | bytes 2752520 | tf_op jit(solution)/shard_map/ppermute | solution.py:359
  19.2 8.4 %collective-permute-start.15 = (bf16[16,8320]{1,0:T(8,128)(2,1)S(1)}, bf16[16,8320]{1,0:T(8,128)(2,1)S(1)}, u32[]{:S(2)}, u32[]{:S(2)}) collective-permute-start(bf16[16,8320]{1,0:T(8,128)(2,1)S(1)} %pad_maximum_fusion.3), channel_id=1, source_target_pairs={{0,4},{1,5},{2,6},{3,7},{4,0},{5,1},{6,2},{7,3},{8,12},{9,13},{10,... | collective-permute-start | bytes 798728 | tf_op jit(solution)/shard_map/ppermute | solution.py:359
  19.7 8.2 %collective-permute-start.18 = (bf16[16,8320]{1,0:T(8,128)(2,1)S(1)}, bf16[16,8320]{1,0:T(8,128)(2,1)S(1)}, u32[]{:S(2)}, u32[]{:S(2)}) collective-permute-start(bf16[16,8320]{1,0:T(8,128)(2,1)S(1)} %pad_maximum_fusion.4), channel_id=1, source_target_pairs={{0,2},{1,3},{2,0},{3,1},{4,6},{5,7},{6,4},{7,5},{8,10},{9,11},{10,... | collective-permute-start | bytes 798728 | tf_op jit(solution)/shard_map/ppermute | solution.py:359
  27.9 3.1 %collective-permute-start.20 = (bf16[32,8320]{1,0:T(8,128)(2,1)S(1)}, bf16[32,8320]{1,0:T(8,128)(2,1)S(1)}, u32[]{:S(2)}, u32[]{:S(2)}) collective-permute-start(bf16[32,8320]{1,0:T(8,128)(2,1)S(1)} %constant_dynamic-update-slice_fusion.refs_1_), channel_id=1, source_target_pairs={{0,1},{1,0},{2,3},{3,2},{4,5},{5,4},{6,7},{7,6},{8,9},{9,8},{10,11... | collective-permute-start | bytes 1597448 | tf_op jit(solution)/shard_map/ppermute | solution.py:359
  28.0 3.1 %collective-permute-start.19 = (bf16[32,8320]{1,0:T(8,128)(2,1)S(1)}, bf16[32,8320]{1,0:T(8,128)(2,1)S(1)}, u32[]{:S(2)}, u32[]{:S(2)}) collective-permute-start(bf16[32,8320]{1,0:T(8,128)(2,1)S(1)} %pad_maximum_fusion.2.refs_0_), channel_id=1, source_target_pairs={{0,1},{1,0},{2,3},{3,2},{4,5},{5,4},{6,7},{7,6},{8,9},{9,8},{10,11... | collective-permute-start | bytes 1597448 | tf_op jit(solution)/shard_map/ppermute | solution.py:359
  29.5 12.6 %collective-permute-start.24 = (bf16[64,3584]{1,0:T(8,128)(2,1)S(1)}, bf16[64,3584]{1,0:T(8,128)(2,1)S(1)}, u32[]{:S(2)}, u32[]{:S(2)}) collective-permute-start(bf16[64,3584]{1,0:T(8,128)(2,1)S(1)} %constant_dynamic-update-slice_fusion.2.refs_2_), channel_id=1, source_target_pairs={{0,16},{16,0},{1,17},{17,1},{2,18},{18,2},{3,19},{19,3},{4,20},{20... | collective-permute-start | bytes 1376264 | tf_op jit(solution)/shard_map/ppermute | solution.py:362
  32.3 3.7 %collective-permute-start.23 = (bf16[128,64]{1,0:T(8,128)(2,1)S(1)}, bf16[128,64]{1,0:T(8,128)(2,1)S(1)}, u32[]{:S(2)}, u32[]{:S(2)}) collective-permute-start(bf16[128,64]{1,0:T(8,128)(2,1)S(1)} %get-tuple-element.287), channel_id=1, source_target_pairs={{0,3},{1,2},{2,1},{3,0},{4,7},{5,6},{6,5},{7,4},{8,11},{9,10},{10,... | collective-permute-start | bytes 49160 | tf_op jit(solution)/shard_map/ppermute | solution.py:359
  33.1 4.0 %collective-permute-start.22 = (bf16[128,64]{1,0:T(8,128)(2,1)S(1)}, bf16[128,64]{1,0:T(8,128)(2,1)S(1)}, u32[]{:S(2)}, u32[]{:S(2)}) collective-permute-start(bf16[128,64]{1,0:T(8,128)(2,1)S(1)} %get-tuple-element.287), channel_id=1, source_target_pairs={{0,2},{1,3},{2,0},{3,1},{4,6},{5,7},{6,4},{7,5},{8,10},{9,11},{10,... | collective-permute-start | bytes 49160 | tf_op jit(solution)/shard_map/ppermute | solution.py:359
  33.8 1.3 %collective-permute-start.21 = (bf16[128,64]{1,0:T(8,128)(2,1)S(1)}, bf16[128,64]{1,0:T(8,128)(2,1)S(1)}, u32[]{:S(2)}, u32[]{:S(2)}) collective-permute-start(bf16[128,64]{1,0:T(8,128)(2,1)S(1)} %get-tuple-element.287), channel_id=1, source_target_pairs={{0,1},{1,0},{2,3},{3,2},{4,5},{5,4},{6,7},{7,6},{8,9},{9,8},{10,11... | collective-permute-start | bytes 49160 | tf_op jit(solution)/shard_map/ppermute | solution.py:359
  37.5 27.7 %collective-permute-start.25 = (bf16[64,1792]{1,0:T(8,128)(2,1)S(1)}, bf16[64,1792]{1,0:T(8,128)(2,1)S(1)}, u32[]{:S(2)}, u32[]{:S(2)}) collective-permute-start(bf16[64,1792]{1,0:T(8,128)(2,1)S(1)} %get-tuple-element.312), channel_id=1, source_target_pairs={{0,4},{1,5},{2,6},{3,7},{4,0},{5,1},{6,2},{7,3},{8,12},{9,13},{10,... | collective-permute-start | bytes 688136 | tf_op jit(solution)/shard_map/ppermute | solution.py:359
  39.0 26.2 %collective-permute-start.28 = (bf16[64,1792]{1,0:T(8,128)(2,1)S(1)}, bf16[64,1792]{1,0:T(8,128)(2,1)S(1)}, u32[]{:S(2)}, u32[]{:S(2)}) collective-permute-start(bf16[64,1792]{1,0:T(8,128)(2,1)S(1)} %get-tuple-element.315), channel_id=1, source_target_pairs={{0,2},{1,3},{2,0},{3,1},{4,6},{5,7},{6,4},{7,5},{8,10},{9,11},{10,... | collective-permute-start | bytes 688136 | tf_op jit(solution)/shard_map/ppermute | solution.py:359
  39.9 25.3 %collective-permute-start.29 = (bf16[64,1792]{1,0:T(8,128)(2,1)S(1)}, bf16[64,1792]{1,0:T(8,128)(2,1)S(1)}, u32[]{:S(2)}, u32[]{:S(2)}) collective-permute-start(bf16[64,1792]{1,0:T(8,128)(2,1)S(1)} %get-tuple-element.316), channel_id=1, source_target_pairs={{0,6},{1,7},{2,4},{3,5},{4,2},{5,3},{6,0},{7,1},{8,14},{9,15},{10,... | collective-permute-start | bytes 688136 | tf_op jit(solution)/shard_map/ppermute | solution.py:359
  42.5 22.8 %copy-start.4 = (bf16[64,3584]{1,0:T(8,128)(2,1)S(1)}, bf16[64,3584]{1,0:T(8,128)(2,1)}, u32[]{:S(2)}) copy-start(bf16[64,3584]{1,0:T(8,128)(2,1)} %copy-done.3) | copy-start | bytes 1376260
  42.5 22.7 %collective-permute-start.26 = (bf16[64,1792]{1,0:T(8,128)(2,1)S(1)}, bf16[64,1792]{1,0:T(8,128)(2,1)S(1)}, u32[]{:S(2)}, u32[]{:S(2)}) collective-permute-start(bf16[64,1792]{1,0:T(8,128)(2,1)S(1)} %get-tuple-element.313), channel_id=1, source_target_pairs={{0,8},{1,9},{2,10},{3,11},{4,12},{5,13},{6,14},{7,15},{8,0},{9,1},... | collective-permute-start | bytes 688136 | tf_op jit(solution)/shard_map/ppermute | solution.py:359
  45.1 20.2 %collective-permute-start.27 = (bf16[64,1792]{1,0:T(8,128)(2,1)S(1)}, bf16[64,1792]{1,0:T(8,128)(2,1)S(1)}, u32[]{:S(2)}, u32[]{:S(2)}) collective-permute-start(bf16[64,1792]{1,0:T(8,128)(2,1)S(1)} %get-tuple-element.314), channel_id=1, source_target_pairs={{0,12},{1,13},{2,14},{3,15},{4,8},{5,9},{6,10},{7,11},{8,4},{9,5},... | collective-permute-start | bytes 688136 | tf_op jit(solution)/shard_map/ppermute | solution.py:359
  (3 other events, 12.9 us)
